TPU v7x, 512 devices: a whole 4x8x8 slice. The times are simulated.
512 devices in a mesh: dp: 64 (over z_hi, y, core), width: 8 (over z_lo, x).
Axes of the slice: x: 4, y: 8, z: 8 (z_hi: 4, z_lo: 2; z = z_hi * 2 + z_lo), core: 2. Of those that a mesh axis runs over, the one named last changes fastest.
Arguments:
- image_emb: bfloat16 [1152, 16384], P('width', 'dp'), may hold values from -0.17675781 to 0.17675781
- text_emb: bfloat16 [1152, 16384], P('width', 'dp'), may hold values from -0.17675781 to 0.17675781
- pair_offsets: int32 [12], replicated, may hold values from 0 to 255
- log_scale: float32 [1], replicated, may hold values from 1.5 to 2.5
- bias: float32 [1], replicated, may hold values from -3 to -1
Outputs:
- image_grad: float32 [1152, 16384], P('width', 'dp')
- text_grad: float32 [1152, 16384], P('width', 'dp')
All inputs are finite; a program needn't handle non-finite values.
Results may differ from a plain program's by a relative error of at most 0.0042.
Values may be sent and summed in bfloat16 or wider, within the bound.
A program may use at most 64 MiB of HBM per device.

v0:
```python
import jax
import jax.numpy as jnp
from jax import lax
from jax.sharding import PartitionSpec as P

CYCLE = 12


EPSILON = 1e-06


def passed_along(value, axis, steps):
    count = lax.axis_size(axis)
    pairs = [(source, (source + steps) % count) for source in range(count)]
    return lax.ppermute(value, axis, pairs)


def tile_product(left, right):
    return lax.dot_general(
        left, right, (((0,), (0,)), ((), ())), preferred_element_type=jnp.float32
    )


def body(image_emb, text_emb, pair_offsets, log_scale, bias):
    img_values = image_emb.astype(jnp.float32)
    txt_values = text_emb.astype(jnp.float32)
    square_sums = lax.psum(
        (jnp.sum(img_values * img_values, axis=0), jnp.sum(txt_values * txt_values, axis=0)),
        "width",
    )
    img_norm = lax.rsqrt(square_sums[0] + EPSILON)[None, :]
    txt_norm = lax.rsqrt(square_sums[1] + EPSILON)[None, :]
    img_unit = img_values * img_norm
    txt_unit = txt_values * txt_norm
    img_low = img_unit.astype(jnp.bfloat16)
    txt_low = txt_unit.astype(jnp.bfloat16)
    temper = jnp.exp(log_scale[0])
    offset_bias = bias[0]
    block_rows = image_emb.shape[1]
    text_now = txt_low
    unit_img_grad = jnp.zeros(img_low.shape, jnp.float32)
    carried = jnp.zeros(text_now.shape, jnp.float32)
    for cycle_step in range(CYCLE):
        if cycle_step > 0:
            text_now = passed_along(text_now, "dp", 1)
            carried = passed_along(carried, "dp", 1)
        logits = lax.psum(tile_product(img_low, text_now), "width")
        row_ids = jnp.arange(logits.shape[0], dtype=jnp.int32)
        col_ids = jnp.arange(logits.shape[1], dtype=jnp.int32)
        row_gap = (row_ids[:, None] - col_ids[None, :]) % block_rows
        positive = (row_gap == pair_offsets[cycle_step]).astype(jnp.float32)
        margin = temper * logits + offset_bias
        slope = (temper * (jax.nn.sigmoid(margin) - positive)).astype(jnp.bfloat16)
        unit_img_grad = unit_img_grad + lax.dot_general(
            text_now, slope, (((1,), (1,)), ((), ())), preferred_element_type=jnp.float32
        )
        text_part = jnp.dot(img_low, slope, preferred_element_type=jnp.float32)
        carried = carried + text_part
    unit_txt_grad = passed_along(carried, "dp", -(CYCLE - 1))
    inner_sums = lax.psum(
        (jnp.sum(img_unit * unit_img_grad, axis=0), jnp.sum(txt_unit * unit_txt_grad, axis=0)),
        "width",
    )
    image_grad = img_norm * (unit_img_grad - img_unit * inner_sums[0][None, :])
    text_grad = txt_norm * (unit_txt_grad - txt_unit * inner_sums[1][None, :])
    return (image_grad, text_grad)


def solution(mesh):
    placed = (P("width", "dp"), P("width", "dp"), P(), P(), P())
    return jax.shard_map(
        body,
        mesh=mesh,
        in_specs=placed,
        out_specs=(P("width", "dp"), P("width", "dp")),
        check_vma=False,
    )
```

profile of v0, /device:TPU:64, one launch (start us, length us, event | category | flops | bytes accessed | tf_op | source)
XLA Modules:
  0.0 415.7 jit_solution(13230696990321161577)
XLA Ops:
  8.2 17.8 %all-reduce.1 = (f32[256]{0:T(256)S(1)}, f32[256]{0:T(256)S(1)}) all-reduce(f32[256]{0:T(256)S(1)} %get-tuple-element.33, f32[256]{0:T(256)S(1)} %get-tuple-element.32), channel_id=1, replica_groups=mesh['dp'=64,'width'=8] {'width'}, use_global_device_ids=true, to_apply=%region_3.0 | all-reduce | flops 512 | bytes 4096 | tf_op jit(solution)/shard_map/psum | solution.py:27
  26.0 1.9 collective-permute-start
  28.9 8.7 %collective-permute-done = bf16[144,256]{1,0:T(8,128)(2,1)S(1)} collective-permute-done((bf16[144,256]{1,0:T(8,128)(2,1)S(1)}, bf16[144,256]{1,0:T(8,128)(2,1)S(1)}, u32[]{:S(2)}, u32[]{:S(2)}) %collective-permute-start) | collective-permute-done | bytes 73760 | tf_op jit(solution)/shard_map/ppermute | solution.py:15
  40.5 7.4 %collective-permute-done.1 = bf16[144,256]{1,0:T(8,128)(2,1)S(1)} collective-permute-done((bf16[144,256]{1,0:T(8,128)(2,1)S(1)}, bf16[144,256]{1,0:T(8,128)(2,1)S(1)}, u32[]{:S(2)}, u32[]{:S(2)}) %collective-permute-start.1) | collective-permute-done | bytes 73760 | tf_op jit(solution)/shard_map/ppermute | solution.py:15
  50.7 7.2 %collective-permute-done.2 = bf16[144,256]{1,0:T(8,128)(2,1)S(1)} collective-permute-done((bf16[144,256]{1,0:T(8,128)(2,1)S(1)}, bf16[144,256]{1,0:T(8,128)(2,1)S(1)}, u32[]{:S(2)}, u32[]{:S(2)}) %collective-permute-start.2) | collective-permute-done | bytes 73760 | tf_op jit(solution)/shard_map/ppermute | solution.py:15
  60.7 7.2 %collective-permute-done.3 = bf16[144,256]{1,0:T(8,128)(2,1)S(1)} collective-permute-done((bf16[144,256]{1,0:T(8,128)(2,1)S(1)}, bf16[144,256]{1,0:T(8,128)(2,1)S(1)}, u32[]{:S(2)}, u32[]{:S(2)}) %collective-permute-start.3) | collective-permute-done | bytes 73760 | tf_op jit(solution)/shard_map/ppermute | solution.py:15
  70.8 7.1 %collective-permute-done.4 = bf16[144,256]{1,0:T(8,128)(2,1)S(1)} collective-permute-done((bf16[144,256]{1,0:T(8,128)(2,1)S(1)}, bf16[144,256]{1,0:T(8,128)(2,1)S(1)}, u32[]{:S(2)}, u32[]{:S(2)}) %collective-permute-start.4) | collective-permute-done | bytes 73760 | tf_op jit(solution)/shard_map/ppermute | solution.py:15
  80.8 7.1 %collective-permute-done.5 = bf16[144,256]{1,0:T(8,128)(2,1)S(1)} collective-permute-done((bf16[144,256]{1,0:T(8,128)(2,1)S(1)}, bf16[144,256]{1,0:T(8,128)(2,1)S(1)}, u32[]{:S(2)}, u32[]{:S(2)}) %collective-permute-start.5) | collective-permute-done | bytes 73760 | tf_op jit(solution)/shard_map/ppermute | solution.py:15
  90.8 7.2 %collective-permute-done.6 = bf16[144,256]{1,0:T(8,128)(2,1)S(1)} collective-permute-done((bf16[144,256]{1,0:T(8,128)(2,1)S(1)}, bf16[144,256]{1,0:T(8,128)(2,1)S(1)}, u32[]{:S(2)}, u32[]{:S(2)}) %collective-permute-start.6) | collective-permute-done | bytes 73760 | tf_op jit(solution)/shard_map/ppermute | solution.py:15
  100.9 7.7 %collective-permute-done.7 = bf16[144,256]{1,0:T(8,128)(2,1)S(1)} collective-permute-done((bf16[144,256]{1,0:T(8,128)(2,1)S(1)}, bf16[144,256]{1,0:T(8,128)(2,1)S(1)}, u32[]{:S(2)}, u32[]{:S(2)}) %collective-permute-start.7) | collective-permute-done | bytes 73760 | tf_op jit(solution)/shard_map/ppermute | solution.py:15
  111.4 7.7 %collective-permute-done.8 = bf16[144,256]{1,0:T(8,128)(2,1)S(1)} collective-permute-done((bf16[144,256]{1,0:T(8,128)(2,1)S(1)}, bf16[144,256]{1,0:T(8,128)(2,1)S(1)}, u32[]{:S(2)}, u32[]{:S(2)}) %collective-permute-start.8) | collective-permute-done | bytes 73760 | tf_op jit(solution)/shard_map/ppermute | solution.py:15
  121.9 7.7 %collective-permute-done.9 = bf16[144,256]{1,0:T(8,128)(2,1)S(1)} collective-permute-done((bf16[144,256]{1,0:T(8,128)(2,1)S(1)}, bf16[144,256]{1,0:T(8,128)(2,1)S(1)}, u32[]{:S(2)}, u32[]{:S(2)}) %collective-permute-start.9) | collective-permute-done | bytes 73760 | tf_op jit(solution)/shard_map/ppermute | solution.py:15
  132.5 7.7 %collective-permute-done.10 = bf16[144,256]{1,0:T(8,128)(2,1)S(1)} collective-permute-done((bf16[144,256]{1,0:T(8,128)(2,1)S(1)}, bf16[144,256]{1,0:T(8,128)(2,1)S(1)}, u32[]{:S(2)}, u32[]{:S(2)}) %collective-permute-start.10) | collective-permute-done | bytes 73760 | tf_op jit(solution)/shard_map/ppermute | solution.py:15
  143.2 99.5 %all-reduce.5.cloned.1.call-done = (f32[256,256]{1,0:T(8,128)}, f32[256,256]{1,0:T(8,128)}, f32[256,256]{1,0:T(8,128)}, f32[256,256]{1,0:T(8,128)}, f32[256,256]...) async-done(((f32[256,256]{1,0:T(8,128)}, ...) | async-done | bytes 3145744 | tf_op jit(solution)/shard_map/psum | solution.py:47
  244.9 1.9 collective-permute-start.11
  260.8 3.5 collective-permute-start.12
  264.5 8.9 %collective-permute-done.12 = f32[144,256]{1,0:T(8,128)S(1)} collective-permute-done((f32[144,256]{1,0:T(8,128)S(1)}, f32[144,256]{1,0:T(8,128)S(1)}, u32[]{:S(2)}, u32[]{:S(2)}) %collective-permute-start.12) | collective-permute-done | bytes 147488 | tf_op jit(solution)/shard_map/ppermute | solution.py:15
  273.4 1.9 collective-permute-start.13
  275.5 9.9 %collective-permute-done.13 = f32[144,256]{1,0:T(8,128)S(1)} collective-permute-done((f32[144,256]{1,0:T(8,128)S(1)}, f32[144,256]{1,0:T(8,128)S(1)}, u32[]{:S(2)}, u32[]{:S(2)}) %collective-permute-start.13) | collective-permute-done | bytes 147488 | tf_op jit(solution)/shard_map/ppermute | solution.py:15
  285.4 1.9 collective-permute-start.14
  287.5 9.5 %collective-permute-done.14 = f32[144,256]{1,0:T(8,128)S(1)} collective-permute-done((f32[144,256]{1,0:T(8,128)S(1)}, f32[144,256]{1,0:T(8,128)S(1)}, u32[]{:S(2)}, u32[]{:S(2)}) %collective-permute-start.14) | collective-permute-done | bytes 147488 | tf_op jit(solution)/shard_map/ppermute | solution.py:15
  297.1 1.9 collective-permute-start.15
  299.2 9.2 %collective-permute-done.15 = f32[144,256]{1,0:T(8,128)S(1)} collective-permute-done((f32[144,256]{1,0:T(8,128)S(1)}, f32[144,256]{1,0:T(8,128)S(1)}, u32[]{:S(2)}, u32[]{:S(2)}) %collective-permute-start.15) | collective-permute-done | bytes 147488 | tf_op jit(solution)/shard_map/ppermute | solution.py:15
  310.5 9.0 %collective-permute-done.16 = f32[144,256]{1,0:T(8,128)S(1)} collective-permute-done((f32[144,256]{1,0:T(8,128)S(1)}, f32[144,256]{1,0:T(8,128)S(1)}, u32[]{:S(2)}, u32[]{:S(2)}) %collective-permute-start.16) | collective-permute-done | bytes 147488 | tf_op jit(solution)/shard_map/ppermute | solution.py:15
  321.6 10.2 %collective-permute-done.17 = f32[144,256]{1,0:T(8,128)S(1)} collective-permute-done((f32[144,256]{1,0:T(8,128)S(1)}, f32[144,256]{1,0:T(8,128)S(1)}, u32[]{:S(2)}, u32[]{:S(2)}) %collective-permute-start.17) | collective-permute-done | bytes 147488 | tf_op jit(solution)/shard_map/ppermute | solution.py:15
  331.8 1.9 collective-permute-start.18
  333.9 10.0 %collective-permute-done.18 = f32[144,256]{1,0:T(8,128)S(1)} collective-permute-done((f32[144,256]{1,0:T(8,128)S(1)}, f32[144,256]{1,0:T(8,128)S(1)}, u32[]{:S(2)}, u32[]{:S(2)}) %collective-permute-start.18) | collective-permute-done | bytes 147488 | tf_op jit(solution)/shard_map/ppermute | solution.py:15
  346.0 9.8 %collective-permute-done.19 = f32[144,256]{1,0:T(8,128)S(1)} collective-permute-done((f32[144,256]{1,0:T(8,128)S(1)}, f32[144,256]{1,0:T(8,128)S(1)}, u32[]{:S(2)}, u32[]{:S(2)}) %collective-permute-start.19) | collective-permute-done | bytes 147488 | tf_op jit(solution)/shard_map/ppermute | solution.py:15
  358.0 9.8 %collective-permute-done.20 = f32[144,256]{1,0:T(8,128)S(1)} collective-permute-done((f32[144,256]{1,0:T(8,128)S(1)}, f32[144,256]{1,0:T(8,128)S(1)}, u32[]{:S(2)}, u32[]{:S(2)}) %collective-permute-start.20) | collective-permute-done | bytes 147488 | tf_op jit(solution)/shard_map/ppermute | solution.py:15
  369.9 9.7 %collective-permute-done.21 = f32[144,256]{1,0:T(8,128)S(1)} collective-permute-done((f32[144,256]{1,0:T(8,128)S(1)}, f32[144,256]{1,0:T(8,128)S(1)}, u32[]{:S(2)}, u32[]{:S(2)}) %collective-permute-start.21) | collective-permute-done | bytes 147488 | tf_op jit(solution)/shard_map/ppermute | solution.py:15
  381.8 7.3 %collective-permute-done.22 = f32[144,256]{1,0:T(8,128)S(1)} collective-permute-done((f32[144,256]{1,0:T(8,128)S(1)}, f32[144,256]{1,0:T(8,128)S(1)}, u32[]{:S(2)}, u32[]{:S(2)}) %collective-permute-start.22) | collective-permute-done | bytes 147488 | tf_op jit(solution)/shard_map/ppermute | solution.py:15
  389.1 18.4 %all-reduce = (f32[256]{0:T(256)S(1)}, f32[256]{0:T(256)S(1)}) all-reduce(f32[256]{0:T(256)S(1)} %get-tuple-element.30, f32[256]{0:T(256)S(1)} %fusion.14), channel_id=1, replica_groups=mesh['dp'=64,'width'=8] {'width'}, use_global_device_ids=true, to_apply=%region_17.18 | all-reduce | flops 512 | bytes 4096 | tf_op jit(solution)/shard_map/psum | solution.py:60
  (112 shorter events, 63.2 us)
Async XLA Ops:
  7.2 18.8 %copy-start.1 = (bf16[144,256]{1,0:T(8,128)(2,1)S(1)}, bf16[144,256]{1,0:T(8,128)(2,1)}, u32[]{:S(2)}) copy-start(bf16[144,256]{1,0:T(8,128)(2,1)} %param.6) | copy-start | bytes 221188
  7.2 235.5 %all-reduce.5.cloned.1.call-start = ((), (), s32[]{:S(2)}) async-start(), calls=%async_computation | async-start | bytes 6291456 | tf_op jit(solution)/shard_map/psum | solution.py:47
  26.0 2.0 copy-start
  26.0 11.6 %collective-permute-start = (bf16[144,256]{1,0:T(8,128)(2,1)S(1)}, bf16[144,256]{1,0:T(8,128)(2,1)S(1)}, u32[]{:S(2)}, u32[]{:S(2)}) collective-permute-start(bf16[144,256]{1,0:T(8,128)(2,1)S(1)} %fusion.6), channel_id=1, source_target_pairs={{0,8},{8,16},{16,24},{24,32},{32,40},{40,48},{48,56},{56,64},{64,7... | collective-permute-start | bytes 221192 | tf_op jit(solution)/shard_map/ppermute | solution.py:15
  37.6 10.2 %collective-permute-start.1 = (bf16[144,256]{1,0:T(8,128)(2,1)S(1)}, bf16[144,256]{1,0:T(8,128)(2,1)S(1)}, u32[]{:S(2)}, u32[]{:S(2)}) collective-permute-start(bf16[144,256]{1,0:T(8,128)(2,1)S(1)} %collective-permute-done), channel_id=1, source_target_pairs={{0,8},{8,16},{16,24},{24,32},{32,40},{40,48},{48,56},{56,64},{64,7... | collective-permute-start | bytes 221192 | tf_op jit(solution)/shard_map/ppermute | solution.py:15
  47.8 10.1 %collective-permute-start.2 = (bf16[144,256]{1,0:T(8,128)(2,1)S(1)}, bf16[144,256]{1,0:T(8,128)(2,1)S(1)}, u32[]{:S(2)}, u32[]{:S(2)}) collective-permute-start(bf16[144,256]{1,0:T(8,128)(2,1)S(1)} %collective-permute-done.1), channel_id=1, source_target_pairs={{0,8},{8,16},{16,24},{24,32},{32,40},{40,48},{48,56},{56,64},{64,7... | collective-permute-start | bytes 221192 | tf_op jit(solution)/shard_map/ppermute | solution.py:15
  57.9 10.1 %collective-permute-start.3 = (bf16[144,256]{1,0:T(8,128)(2,1)S(1)}, bf16[144,256]{1,0:T(8,128)(2,1)S(1)}, u32[]{:S(2)}, u32[]{:S(2)}) collective-permute-start(bf16[144,256]{1,0:T(8,128)(2,1)S(1)} %collective-permute-done.2), channel_id=1, source_target_pairs={{0,8},{8,16},{16,24},{24,32},{32,40},{40,48},{48,56},{56,64},{64,7... | collective-permute-start | bytes 221192 | tf_op jit(solution)/shard_map/ppermute | solution.py:15
  68.0 10.0 %collective-permute-start.4 = (bf16[144,256]{1,0:T(8,128)(2,1)S(1)}, bf16[144,256]{1,0:T(8,128)(2,1)S(1)}, u32[]{:S(2)}, u32[]{:S(2)}) collective-permute-start(bf16[144,256]{1,0:T(8,128)(2,1)S(1)} %collective-permute-done.3), channel_id=1, source_target_pairs={{0,8},{8,16},{16,24},{24,32},{32,40},{40,48},{48,56},{56,64},{64,7... | collective-permute-start | bytes 221192 | tf_op jit(solution)/shard_map/ppermute | solution.py:15
  78.0 10.0 %collective-permute-start.5 = (bf16[144,256]{1,0:T(8,128)(2,1)S(1)}, bf16[144,256]{1,0:T(8,128)(2,1)S(1)}, u32[]{:S(2)}, u32[]{:S(2)}) collective-permute-start(bf16[144,256]{1,0:T(8,128)(2,1)S(1)} %collective-permute-done.4), channel_id=1, source_target_pairs={{0,8},{8,16},{16,24},{24,32},{32,40},{40,48},{48,56},{56,64},{64,7... | collective-permute-start | bytes 221192 | tf_op jit(solution)/shard_map/ppermute | solution.py:15
  88.0 10.0 %collective-permute-start.6 = (bf16[144,256]{1,0:T(8,128)(2,1)S(1)}, bf16[144,256]{1,0:T(8,128)(2,1)S(1)}, u32[]{:S(2)}, u32[]{:S(2)}) collective-permute-start(bf16[144,256]{1,0:T(8,128)(2,1)S(1)} %collective-permute-done.5), channel_id=1, source_target_pairs={{0,8},{8,16},{16,24},{24,32},{32,40},{40,48},{48,56},{56,64},{64,7... | collective-permute-start | bytes 221192 | tf_op jit(solution)/shard_map/ppermute | solution.py:15
  98.0 10.5 %collective-permute-start.7 = (bf16[144,256]{1,0:T(8,128)(2,1)S(1)}, bf16[144,256]{1,0:T(8,128)(2,1)S(1)}, u32[]{:S(2)}, u32[]{:S(2)}) collective-permute-start(bf16[144,256]{1,0:T(8,128)(2,1)S(1)} %collective-permute-done.6), channel_id=1, source_target_pairs={{0,8},{8,16},{16,24},{24,32},{32,40},{40,48},{48,56},{56,64},{64,7... | collective-permute-start | bytes 221192 | tf_op jit(solution)/shard_map/ppermute | solution.py:15
  108.5 10.5 %collective-permute-start.8 = (bf16[144,256]{1,0:T(8,128)(2,1)S(1)}, bf16[144,256]{1,0:T(8,128)(2,1)S(1)}, u32[]{:S(2)}, u32[]{:S(2)}) collective-permute-start(bf16[144,256]{1,0:T(8,128)(2,1)S(1)} %collective-permute-done.7), channel_id=1, source_target_pairs={{0,8},{8,16},{16,24},{24,32},{32,40},{40,48},{48,56},{56,64},{64,7... | collective-permute-start | bytes 221192 | tf_op jit(solution)/shard_map/ppermute | solution.py:15
  119.1 10.5 %collective-permute-start.9 = (bf16[144,256]{1,0:T(8,128)(2,1)S(1)}, bf16[144,256]{1,0:T(8,128)(2,1)S(1)}, u32[]{:S(2)}, u32[]{:S(2)}) collective-permute-start(bf16[144,256]{1,0:T(8,128)(2,1)S(1)} %collective-permute-done.8), channel_id=1, source_target_pairs={{0,8},{8,16},{16,24},{24,32},{32,40},{40,48},{48,56},{56,64},{64,7... | collective-permute-start | bytes 221192 | tf_op jit(solution)/shard_map/ppermute | solution.py:15
  129.6 10.5 %collective-permute-start.10 = (bf16[144,256]{1,0:T(8,128)(2,1)S(1)}, bf16[144,256]{1,0:T(8,128)(2,1)S(1)}, u32[]{:S(2)}, u32[]{:S(2)}) collective-permute-start(bf16[144,256]{1,0:T(8,128)(2,1)S(1)} %collective-permute-done.9), channel_id=1, source_target_pairs={{0,8},{8,16},{16,24},{24,32},{32,40},{40,48},{48,56},{56,64},{64,7... | collective-permute-start | bytes 221192 | tf_op jit(solution)/shard_map/ppermute | solution.py:15
  244.7 2.1 copy-start.11
  244.9 14.9 %collective-permute-start.11 = (f32[144,256]{1,0:T(8,128)S(1)}, f32[144,256]{1,0:T(8,128)S(1)}, u32[]{:S(2)}, u32[]{:S(2)}) collective-permute-start(f32[144,256]{1,0:T(8,128)S(1)} %fusion.39), channel_id=1, source_target_pairs={{0,8},{8,16},{16,24},{24,32},{32,40},{40,48},{48,56},{56,64},{64,7... | collective-permute-start | bytes 442376 | tf_op jit(solution)/shard_map/ppermute | solution.py:15
  246.8 1.0 copy-start.10
  248.7 1.0 copy-start.8
  253.5 1.0 copy-start.3
  254.4 1.0 copy-start.13
  258.0 1.0 copy-start.2
  260.8 12.6 %collective-permute-start.12 = (f32[144,256]{1,0:T(8,128)S(1)}, f32[144,256]{1,0:T(8,128)S(1)}, u32[]{:S(2)}, u32[]{:S(2)}) collective-permute-start(f32[144,256]{1,0:T(8,128)S(1)} %convolution_add_fusion), channel_id=1, source_target_pairs={{0,8},{8,16},{16,24},{24,32},{32,40},{40,48},{48,56},{56,64},{64,7... | collective-permute-start | bytes 442376 | tf_op jit(solution)/shard_map/ppermute | solution.py:15
  273.4 12.0 %collective-permute-start.13 = (f32[144,256]{1,0:T(8,128)S(1)}, f32[144,256]{1,0:T(8,128)S(1)}, u32[]{:S(2)}, u32[]{:S(2)}) collective-permute-start(f32[144,256]{1,0:T(8,128)S(1)} %add.280), channel_id=1, source_target_pairs={{0,8},{8,16},{16,24},{24,32},{32,40},{40,48},{48,56},{56,64},{64,7... | collective-permute-start | bytes 442376 | tf_op jit(solution)/shard_map/ppermute | solution.py:15
  285.4 11.6 %collective-permute-start.14 = (f32[144,256]{1,0:T(8,128)S(1)}, f32[144,256]{1,0:T(8,128)S(1)}, u32[]{:S(2)}, u32[]{:S(2)}) collective-permute-start(f32[144,256]{1,0:T(8,128)S(1)} %add.281), channel_id=1, source_target_pairs={{0,8},{8,16},{16,24},{24,32},{32,40},{40,48},{48,56},{56,64},{64,7... | collective-permute-start | bytes 442376 | tf_op jit(solution)/shard_map/ppermute | solution.py:15
  297.1 11.3 %collective-permute-start.15 = (f32[144,256]{1,0:T(8,128)S(1)}, f32[144,256]{1,0:T(8,128)S(1)}, u32[]{:S(2)}, u32[]{:S(2)}) collective-permute-start(f32[144,256]{1,0:T(8,128)S(1)} %add.282), channel_id=1, source_target_pairs={{0,8},{8,16},{16,24},{24,32},{32,40},{40,48},{48,56},{56,64},{64,7... | collective-permute-start | bytes 442376 | tf_op jit(solution)/shard_map/ppermute | solution.py:15
  308.4 11.1 %collective-permute-start.16 = (f32[144,256]{1,0:T(8,128)S(1)}, f32[144,256]{1,0:T(8,128)S(1)}, u32[]{:S(2)}, u32[]{:S(2)}) collective-permute-start(f32[144,256]{1,0:T(8,128)S(1)} %add.283), channel_id=1, source_target_pairs={{0,8},{8,16},{16,24},{24,32},{32,40},{40,48},{48,56},{56,64},{64,7... | collective-permute-start | bytes 442376 | tf_op jit(solution)/shard_map/ppermute | solution.py:15
  319.5 12.3 %collective-permute-start.17 = (f32[144,256]{1,0:T(8,128)S(1)}, f32[144,256]{1,0:T(8,128)S(1)}, u32[]{:S(2)}, u32[]{:S(2)}) collective-permute-start(f32[144,256]{1,0:T(8,128)S(1)} %add.284), channel_id=1, source_target_pairs={{0,8},{8,16},{16,24},{24,32},{32,40},{40,48},{48,56},{56,64},{64,7... | collective-permute-start | bytes 442376 | tf_op jit(solution)/shard_map/ppermute | solution.py:15
  331.8 12.1 %collective-permute-start.18 = (f32[144,256]{1,0:T(8,128)S(1)}, f32[144,256]{1,0:T(8,128)S(1)}, u32[]{:S(2)}, u32[]{:S(2)}) collective-permute-start(f32[144,256]{1,0:T(8,128)S(1)} %add.285), channel_id=1, source_target_pairs={{0,8},{8,16},{16,24},{24,32},{32,40},{40,48},{48,56},{56,64},{64,7... | collective-permute-start | bytes 442376 | tf_op jit(solution)/shard_map/ppermute | solution.py:15
  343.9 11.9 %collective-permute-start.19 = (f32[144,256]{1,0:T(8,128)S(1)}, f32[144,256]{1,0:T(8,128)S(1)}, u32[]{:S(2)}, u32[]{:S(2)}) collective-permute-start(f32[144,256]{1,0:T(8,128)S(1)} %add.286), channel_id=1, source_target_pairs={{0,8},{8,16},{16,24},{24,32},{32,40},{40,48},{48,56},{56,64},{64,7... | collective-permute-start | bytes 442376 | tf_op jit(solution)/shard_map/ppermute | solution.py:15
  355.9 11.9 %collective-permute-start.20 = (f32[144,256]{1,0:T(8,128)S(1)}, f32[144,256]{1,0:T(8,128)S(1)}, u32[]{:S(2)}, u32[]{:S(2)}) collective-permute-start(f32[144,256]{1,0:T(8,128)S(1)} %add.287), channel_id=1, source_target_pairs={{0,8},{8,16},{16,24},{24,32},{32,40},{40,48},{48,56},{56,64},{64,7... | collective-permute-start | bytes 442376 | tf_op jit(solution)/shard_map/ppermute | solution.py:15
  367.8 11.8 %collective-permute-start.21 = (f32[144,256]{1,0:T(8,128)S(1)}, f32[144,256]{1,0:T(8,128)S(1)}, u32[]{:S(2)}, u32[]{:S(2)}) collective-permute-start(f32[144,256]{1,0:T(8,128)S(1)} %add.288), channel_id=1, source_target_pairs={{0,8},{8,16},{16,24},{24,32},{32,40},{40,48},{48,56},{56,64},{64,7... | collective-permute-start | bytes 442376 | tf_op jit(solution)/shard_map/ppermute | solution.py:15
  379.6 9.5 %collective-permute-start.22 = (f32[144,256]{1,0:T(8,128)S(1)}, f32[144,256]{1,0:T(8,128)S(1)}, u32[]{:S(2)}, u32[]{:S(2)}) collective-permute-start(f32[144,256]{1,0:T(8,128)S(1)} %add.289), channel_id=1, source_target_pairs={{0,424},{8,432},{16,440},{24,448},{32,456},{40,464},{48,472},{56,4... | collective-permute-start | bytes 442376 | tf_op jit(solution)/shard_map/ppermute | solution.py:15
  (6 other events, 5.4 us)
Sparse Core Ops, SparseCore 0:
  141.2 101.4 all-reduce.4
where the time goes:
time: 417 us; the launch traced here: 416 us
  waiting for transfers between devices  286 us (69%)
  starting transfers between devices  45.7 us (11%)
  blocking collectives  36.2 us (9%)
  matrix products  17.4 us (4%)
  between operations  15.8 us (4%)
  other arithmetic  12.7 us (3%)
    ppermute x23, waiting for transfers between devices, passed_along(): return lax.ppermute(value, axis, pairs)  186 us
    psum x1, waiting for transfers between devices, body(): logits = lax.psum(tile_product(img_low, text_now), 'width')  99.5 us
    ppermute x23, starting transfers between devices, passed_along(): return lax.ppermute(value, axis, pairs)  45.6 us
    psum x1, blocking collectives, body(): lax.psum((jnp.sum(img_unit * unit_img_grad, axis=0), jnp.sum(txt_unit * u...  18.4 us
    psum x1, blocking collectives, body(): lax.psum((jnp.sum(img_values * img_values, axis=0), jnp.sum(txt_values *...  17.8 us
    dot_general x12, matrix products, tile_product(): lax.dot_general(left, right, (((0,), (0,)), ((), ())), preferred_element_...  11.3 us
    convert_element_type x11, other arithmetic, body(): slope = (temper * (jax.nn.sigmoid(margin) - positive)).astype(jnp.bfloat16)  10.1 us
  transfers between devices with their start and end apart: 24, of which 23 were waited for; matrix products, arithmetic and copies ran while one was open for 6% of the time, Pallas kernels for 0%

commit v1 on v0

v1 whole, which is shorter than its diff:
```python
import functools

import jax
import jax.numpy as jnp
from jax import lax
from jax.experimental import pallas as pl
from jax.experimental.pallas import tpu as pltpu
from jax.sharding import PartitionSpec as P

MESH = pl.DeviceIdType.MESH
F32 = jnp.float32
BF16 = jnp.bfloat16
EPSILON = 1e-06
CYCLE = 12
NW = 8
FEAT = 144
MAIN = 128
TAIL = FEAT - MAIN
D = NW * FEAT
COLS = 256
ROWS = COLS // NW
REACH = 6
ORDER = (0, 2, 5, 1, 3, 4, 6)
PLACE = {d: i for i, d in enumerate(ORDER)}


def rows_of(d):
    return pl.ds(PLACE[d] * ROWS, ROWS)


def kernel(
    chips,
    img_hbm,
    txt_hbm,
    offsets,
    log_scale,
    bias,
    img_out,
    txt_out,
    img_raw,
    txt_in,
    txt_wide,
    a_send,
    a_recv,
    low,
    txt,
    unit,
    tnorm,
    slopes,
    dots,
    own_grad,
    f_send,
    f_recv,
    p_send,
    p_recv,
    p_own,
    e_send,
    e_recv,
    g_send,
    g_recv,
    local_sem,
    a_ss,
    a_rs,
    b_ss,
    b_rs,
    c_ss,
    c_rs,
    f_ss,
    f_rs,
    e_ss,
    e_rs,
    g_ss,
    g_rs,
    s_ss,
    s_rs,
):
    dp = lax.axis_index("dp")
    w = lax.axis_index("width")
    chip = lax.div(dp, 2)
    core = lax.rem(dp, 2)

    def along(d):
        return (lax.rem(chip + d + chips, chips) * 2 + core, w)

    def across(j):
        return (dp, lax.rem(w + j, NW))

    other = (dp + 1 - 2 * core, w)

    def remote(src, dst, ss, rs, to):
        return pltpu.make_async_remote_copy(
            src_ref=src, dst_ref=dst, send_sem=ss, recv_sem=rs, device_id=to, device_id_type=MESH
        )

    barrier = pltpu.get_barrier_semaphore()
    peers = [across(j) for j in range(1, NW)] + [other]
    peers += [along(d) for d in range(-REACH, REACH + 1) if d != 0]
    for peer in peers:
        pl.semaphore_signal(barrier, inc=1, device_id=peer, device_id_type=MESH)

    get_txt = pltpu.make_async_copy(txt_hbm, txt_in, local_sem.at[0])
    get_img = pltpu.make_async_copy(img_hbm, img_raw.at[w], local_sem.at[1])
    get_txt.start()
    get_img.start()

    @pl.when(core == 0)
    def _():
        txt[rows_of(REACH), :] = jnp.zeros((ROWS, D), BF16)

    txt_wide[FEAT:, :] = jnp.zeros((COLS - FEAT, COLS), F32)
    dots[...] = jnp.zeros(dots.shape, F32)
    get_txt.wait()
    txt_wide[:FEAT, :] = txt_in[...].astype(F32)
    a_send[...] = txt_wide[...].T.astype(BF16).reshape(NW, ROWS, COLS)
    get_img.wait()
    pl.semaphore_wait(barrier, len(peers))

    a_copies = []
    for j in range(1, NW):
        copy = remote(a_send.at[lax.rem(w + j, NW)], a_recv.at[w], a_ss.at[j], a_rs.at[j], across(j))
        copy.start()
        a_copies.append(copy)
    b_copies = []
    for j in range(1, NW):
        copy = remote(img_raw.at[w], img_raw.at[w], b_ss.at[j], b_rs.at[j], across(j))
        copy.start()
        b_copies.append(copy)
    a_recv[w] = a_send[w]
    for copy in a_copies:
        copy.wait_recv()

    tail = jnp.zeros((ROWS, MAIN), F32)
    for v in range(NW):
        piece = a_recv[v].astype(F32)
        unit[:, v * MAIN : (v + 1) * MAIN] = piece[:, :MAIN]
        rest = piece[:, MAIN:]
        tail = tail + (pltpu.roll(rest, v * TAIL, 1) if v else rest)
    unit[:, NW * MAIN :] = tail
    raw = unit[...]
    norm = lax.rsqrt(jnp.sum(raw * raw, axis=1, keepdims=True) + EPSILON)
    scaled = raw * norm
    unit[...] = scaled
    tnorm[...] = jnp.broadcast_to(norm, tnorm.shape)
    txt[rows_of(0), :] = scaled.astype(BF16)

    def pass_text(src, dst, to):
        return remote(txt.at[rows_of(src)], txt.at[rows_of(dst)], c_ss.at[dst], c_rs.at[dst], to)

    to2 = pass_text(0, 2, along(2))
    to5 = pass_text(0, 5, along(5))
    to5.start()
    to2.start()

    total = jnp.sum(jnp.square(img_raw[w].astype(F32)), axis=0, keepdims=True)
    for j, copy in enumerate(b_copies, 1):
        copy.wait_recv()
        total = total + jnp.sum(jnp.square(img_raw[lax.rem(w - j + NW, NW)].astype(F32)), axis=0, keepdims=True)
    inorm = lax.rsqrt(total + EPSILON)
    for v in range(NW):
        scaled = (img_raw[v].astype(F32) * inorm).astype(BF16)
        low[core, v * MAIN : (v + 1) * MAIN, :] = scaled[:MAIN]
        low[core, NW * MAIN + v * TAIL : NW * MAIN + (v + 1) * TAIL, :] = scaled[MAIN:]
    share = remote(low.at[core], low.at[core], s_ss.at[0], s_rs.at[0], other)
    share.start()

    temper = jnp.exp(jnp.full((1, COLS), log_scale[0], F32))
    shift = bias[0]
    col = lax.broadcasted_iota(jnp.int32, (ROWS, COLS), 1)
    row = lax.broadcasted_iota(jnp.int32, (ROWS, COLS), 0) + w * ROWS
    gap = col - row

    def back(d):
        return remote(f_send.at[d], f_recv.at[d], f_ss.at[d], f_rs.at[d], along(-d))

    def meet(ds):
        first = PLACE[ds[0]] * ROWS
        size = len(ds) * ROWS
        here = txt[first : first + size, :]
        grad = jnp.zeros((size, D), F32)
        for i in range(2):
            logits = jnp.dot(here, low[i], preferred_element_type=F32)
            parts = []
            dot = jnp.zeros((1, COLS), F32)
            for n, d in enumerate(ds):
                step = 2 * d + i - core
                met = jnp.logical_and(step >= 0, step < CYCLE).astype(F32)
                offset = offsets[jnp.clip(step, 0, CYCLE - 1)]
                own = logits[n * ROWS : (n + 1) * ROWS]
                positive = (((gap - offset) & (COLS - 1)) == 0).astype(F32)
                slope = (temper * (jax.nn.sigmoid(temper * own + shift) - positive)) * met
                slope = slope.astype(BF16)
                dot = dot + jnp.sum(slope.astype(F32) * own, axis=0, keepdims=True)
                slopes[i, (PLACE[d]) * ROWS : (PLACE[d] + 1) * ROWS, :] = slope
                parts.append(slope)
            dots[i] = dots[i] + jnp.broadcast_to(dot, dots.shape[1:])
            grad = grad + lax.dot_general(
                slopes[i, first : first + size, :], low[i], (((1,), (1,)), ((), ())), preferred_element_type=F32
            )
        for n, d in enumerate(ds):
            part = grad[n * ROWS : (n + 1) * ROWS]
            if d == 0:
                own_grad[...] = part
            else:
                f_send[d] = part.astype(BF16)

    share.wait_recv()
    meet((0,))
    to2.wait_recv()
    to1 = pass_text(2, 1, along(-1))
    to3 = pass_text(2, 3, along(1))
    to1.start()
    to3.start()
    to5.wait_recv()
    to4 = pass_text(5, 4, along(-1))
    to6 = pass_text(5, 6, along(1))
    to4.start()

    @pl.when(core == 1)
    def _():
        to6.start()

    meet((2, 5))
    for d in (5, 2):
        back(d).start()
    to1.wait_recv()
    to3.wait_recv()
    to4.wait_recv()

    @pl.when(core == 1)
    def _():
        to6.wait_recv()

    meet((1, 3, 4, 6))
    for d in (4, 3, 1):
        back(d).start()

    @pl.when(core == 1)
    def _():
        back(6).start()

    def image_part(i, store):
        third = D // 3
        dot = dots[i][:1]
        for t in range(3):
            part = lax.dot_general(
                txt[:, t * third : (t + 1) * third], slopes[i], (((0,), (0,)), ((), ())), preferred_element_type=F32
            )
            part = part - low[i, t * third : (t + 1) * third, :].astype(F32) * dot
            for u in range(3):
                v = 3 * t + u
                chunk = part[u * MAIN : (u + 1) * MAIN]
                if v < NW:
                    store(v, 0, MAIN, chunk)
                else:
                    for q in range(NW):
                        store(q, MAIN, FEAT, chunk[q * TAIL : (q + 1) * TAIL])

    def to_other(v, lo, hi, chunk):
        p_send[v, lo:hi, :] = chunk.astype(BF16)

    def to_own(v, lo, hi, chunk):
        p_own[v, lo:hi, :] = chunk

    image_part(1 - core, to_other)
    pair = remote(p_send, p_recv, s_ss.at[1], s_rs.at[1], other)
    pair.start()
    image_part(core, to_own)
    pair.wait_recv()
    for v in range(NW):
        p_own[v] = p_own[v] + p_recv[v].astype(F32)
        e_send[v] = p_own[v].astype(BF16)
    e_copies = []
    for j in range(1, NW):
        copy = remote(e_send.at[lax.rem(w + j, NW)], e_recv.at[j], e_ss.at[j], e_rs.at[j], across(j))
        copy.start()
        e_copies.append(copy)

    grad = own_grad[...]
    for d in (2, 5, 1, 3, 4):
        back(d).wait_recv()
        grad = grad + f_recv[d].astype(F32)
    own_grad[...] = grad

    @pl.when(core == 1)
    def _():
        back(6).wait_recv()
        own_grad[...] = own_grad[...] + f_recv[6].astype(F32)

    grad = own_grad[...]
    scaled = unit[...]
    dot = jnp.sum(scaled * grad, axis=1, keepdims=True)
    final = tnorm[:, :1] * (grad - scaled * dot)
    tail = final[:, NW * MAIN :]
    for v in range(NW):
        g_send[v, :, :MAIN] = final[:, v * MAIN : (v + 1) * MAIN]
        g_send[v, :, MAIN:] = pltpu.roll(tail, MAIN - v * TAIL, 1) if v else tail
    g_copies = []
    for j in range(1, NW):
        copy = remote(g_send.at[lax.rem(w + j, NW)], g_recv.at[w], g_ss.at[j], g_rs.at[j], across(j))
        copy.start()
        g_copies.append(copy)
    g_recv[w] = g_send[w]

    grad = p_own[w]
    for j, copy in enumerate(e_copies, 1):
        copy.wait_recv()
        grad = grad + e_recv[j].astype(F32)
    img_out[...] = grad * inorm
    for copy in g_copies:
        copy.wait_recv()
    txt_out[...] = g_recv[...].reshape(COLS, COLS).T[:FEAT]

    for copy in a_copies + b_copies + e_copies + g_copies:
        copy.wait_send()
    for copy in (to1, to2, to3, to4, to5, share, pair):
        copy.wait_send()
    for d in range(1, REACH):
        back(d).wait_send()

    @pl.when(core == 1)
    def _():
        to6.wait_send()
        back(6).wait_send()


def solution(mesh):
    chips = mesh.shape["dp"] // 2
    slots = len(ORDER)
    dma = pltpu.SemaphoreType.DMA

    def body(image_emb, text_emb, pair_offsets, log_scale, bias):
        shape = jax.ShapeDtypeStruct((FEAT, COLS), F32)
        any_space = pl.BlockSpec(memory_space=pl.ANY)
        smem = pl.BlockSpec(memory_space=pltpu.SMEM)
        vmem = pl.BlockSpec(memory_space=pltpu.VMEM)
        return pl.pallas_call(
            functools.partial(kernel, chips),
            out_shape=(shape, shape),
            in_specs=[any_space, any_space, smem, smem, smem],
            out_specs=(vmem, vmem),
            scratch_shapes=[
                pltpu.VMEM((NW, FEAT, COLS), BF16),
                pltpu.VMEM((FEAT, COLS), BF16),
                pltpu.VMEM((COLS, COLS), F32),
                pltpu.VMEM((NW, ROWS, COLS), BF16),
                pltpu.VMEM((NW, ROWS, COLS), BF16),
                pltpu.VMEM((2, D, COLS), BF16),
                pltpu.VMEM((slots * ROWS, D), BF16),
                pltpu.VMEM((ROWS, D), F32),
                pltpu.VMEM((ROWS, MAIN), F32),
                pltpu.VMEM((2, slots * ROWS, COLS), BF16),
                pltpu.VMEM((2, 8, COLS), F32),
                pltpu.VMEM((ROWS, D), F32),
                pltpu.VMEM((slots, ROWS, D), BF16),
                pltpu.VMEM((slots, ROWS, D), BF16),
                pltpu.VMEM((NW, FEAT, COLS), BF16),
                pltpu.VMEM((NW, FEAT, COLS), BF16),
                pltpu.VMEM((NW, FEAT, COLS), F32),
                pltpu.VMEM((NW, FEAT, COLS), BF16),
                pltpu.VMEM((NW, FEAT, COLS), BF16),
                pltpu.VMEM((NW, ROWS, COLS), F32),
                pltpu.VMEM((NW, ROWS, COLS), F32),
                dma((2,)),
                dma((NW,)),
                dma((NW,)),
                dma((NW,)),
                dma((NW,)),
                dma((slots,)),
                dma((slots,)),
                dma((slots,)),
                dma((slots,)),
                dma((NW,)),
                dma((NW,)),
                dma((NW,)),
                dma((NW,)),
                dma((2,)),
                dma((2,)),
            ],
            compiler_params=pltpu.CompilerParams(
                collective_id=0, has_side_effects=True, vmem_limit_bytes=40 * 1024 * 1024
            ),
        )(image_emb, text_emb, pair_offsets, log_scale, bias)

    placed = (P("width", "dp"), P("width", "dp"), P(), P(), P())
    return jax.shard_map(
        body,
        mesh=mesh,
        in_specs=placed,
        out_specs=(P("width", "dp"), P("width", "dp")),
        check_vma=False,
    )
```

time: 417 us -> 69.7 us (0.17)
  the two profiles are of different devices: /device:TPU:64 before, /device:TPU:56 now
where the time goes in v1:
time: 69.7 us; the launch traced here: 69.5 us
  Pallas kernels  64.5 us (93%)
  local copies, waits for them, and re-layouts  3.09 us (4%)
  between operations  1.97 us (3%)
    pallas_call x1, Pallas kernels, body(): pl.pallas_call(functools.partial(kernel, chips), out_shape=(shape, shape)...  64.5 us
    unnamed x8, local copies, waits for them, and re-layouts  3.09 us

profile of v1, /device:TPU:56, one launch (start us, length us, event | category | flops | bytes accessed | tf_op | source)
XLA Modules:
  0.0 69.5 jit_solution(2869471127948388865)
XLA Ops:
  1.3 0.0 copy-start.2
  1.9 0.0 copy-done.2
  2.0 0.0 copy-start
  2.0 0.9 %copy-done = bf16[144,256]{1,0:T(8,128)(2,1)S(1)} copy-done((bf16[144,256]{1,0:T(8,128)(2,1)S(1)}, bf16[144,256]{1,0:T(8,128)(2,1)}, u32[]{:S(2)}) %copy-start) | copy-done | bytes 73752
  2.8 0.0 copy-start.1
  2.8 0.9 %copy-done.1 = bf16[144,256]{1,0:T(8,128)(2,1)S(1)} copy-done((bf16[144,256]{1,0:T(8,128)(2,1)S(1)}, bf16[144,256]{1,0:T(8,128)(2,1)}, u32[]{:S(2)}) %copy-start.1) | copy-done | bytes 73752
  3.7 64.5 %shard_map.68 = (f32[144,256]{1,0:T(8,128)S(1)}, f32[144,256]{1,0:T(8,128)S(1)}) custom-call(bf16[144,256]{1,0:T(8,128)(2,1)S(1)} %copy-done, bf16[144,256]{1,0:T(8,128)(2,1)S(1)} %copy-done.1, s32[12]{0:T(128)S(1)} %copy-done.2, f32[1]{0:T(128)S(6)} %copy.9.log_scale, f32[1]{0:T(128)S(6)} %copy.10.bias), custom_call_target="tpu_custom_call" | custom-call | tf_op jit(solution)/shard_map/pallas_call | solution.py:336
  68.2 0.7 copy.11
  68.9 0.7 copy.12
Async XLA Ops:
  1.3 0.7 copy-start.2
  2.0 0.9 %copy-start = (bf16[144,256]{1,0:T(8,128)(2,1)S(1)}, bf16[144,256]{1,0:T(8,128)(2,1)}, u32[]{:S(2)}) copy-start(bf16[144,256]{1,0:T(8,128)(2,1)} %img_hbm.1) | copy-start | bytes 221188
  2.8 0.9 %copy-start.1 = (bf16[144,256]{1,0:T(8,128)(2,1)S(1)}, bf16[144,256]{1,0:T(8,128)(2,1)}, u32[]{:S(2)}) copy-start(bf16[144,256]{1,0:T(8,128)(2,1)} %txt_hbm.1) | copy-start | bytes 221188

commit v2 on v1

--- a/solution.py
+++ b/solution.py
@@ -13,6 +13,7 @@
 EPSILON = 1e-06
 CYCLE = 12
 NW = 8
+NX = 4
 FEAT = 144
 MAIN = 128
 TAIL = FEAT - MAIN
@@ -48,7 +49,6 @@
     tnorm,
     slopes,
     dots,
-    own_grad,
     f_send,
     f_recv,
     p_send,
@@ -56,6 +56,9 @@
     p_own,
     e_send,
     e_recv,
+    z_send,
+    z_recv,
+    keep,
     g_send,
     g_recv,
     local_sem,
@@ -73,6 +76,8 @@
     g_rs,
     s_ss,
     s_rs,
+    z_ss,
+    z_rs,
 ):
     dp = lax.axis_index("dp")
     w = lax.axis_index("width")
@@ -86,6 +91,14 @@
         return (dp, lax.rem(w + j, NW))
 
     other = (dp + 1 - 2 * core, w)
+    x = lax.rem(w, NX)
+    base = w - x
+    base2 = NX - base
+    w2 = base2 + x
+    partner = (dp, w2)
+
+    def near(j):
+        return lax.rem(x + j, NX)
 
     def remote(src, dst, ss, rs, to):
         return pltpu.make_async_remote_copy(
@@ -120,14 +133,16 @@
         copy = remote(a_send.at[lax.rem(w + j, NW)], a_recv.at[w], a_ss.at[j], a_rs.at[j], across(j))
         copy.start()
         a_copies.append(copy)
-    b_copies = []
-    for j in range(1, NW):
-        copy = remote(img_raw.at[w], img_raw.at[w], b_ss.at[j], b_rs.at[j], across(j))
-        copy.start()
-        b_copies.append(copy)
     a_recv[w] = a_send[w]
     for copy in a_copies:
         copy.wait_recv()
+    z_copy = remote(img_raw.at[w], img_raw.at[w], b_ss.at[0], b_rs.at[0], partner)
+    z_copy.start()
+    b_copies = []
+    for j in (1, 3, 2):
+        copy = remote(img_raw.at[w], img_raw.at[w], b_ss.at[j], b_rs.at[j], (dp, base + near(j)))
+        copy.start()
+        b_copies.append(copy)
 
     tail = jnp.zeros((ROWS, MAIN), F32)
     for v in range(NW):
@@ -151,10 +166,20 @@
     to5.start()
     to2.start()
 
-    total = jnp.sum(jnp.square(img_raw[w].astype(F32)), axis=0, keepdims=True)
-    for j, copy in enumerate(b_copies, 1):
+    z_copy.wait_recv()
+    for j in (1, 3, 2):
+        copy = remote(img_raw.at[w2], img_raw.at[w2], b_ss.at[NX + j], b_rs.at[NX + j], (dp, base + near(j)))
+        copy.start()
+        b_copies.append(copy)
+
+    def squares(v):
+        return jnp.sum(jnp.square(img_raw[v].astype(F32)), axis=0, keepdims=True)
+
+    total = squares(w) + squares(w2)
+    for n, copy in enumerate(b_copies):
         copy.wait_recv()
-        total = total + jnp.sum(jnp.square(img_raw[lax.rem(w - j + NW, NW)].astype(F32)), axis=0, keepdims=True)
+        j = (1, 3, 2)[n % 3]
+        total = total + squares((base if n < 3 else base2) + near(NX - j))
     inorm = lax.rsqrt(total + EPSILON)
     for v in range(NW):
         scaled = (img_raw[v].astype(F32) * inorm).astype(BF16)
@@ -169,8 +194,10 @@
     row = lax.broadcasted_iota(jnp.int32, (ROWS, COLS), 0) + w * ROWS
     gap = col - row
 
+    home = {1: 1, 3: -1, 4: 1, 6: -1, 2: -2, 5: -5}
+
     def back(d):
-        return remote(f_send.at[d], f_recv.at[d], f_ss.at[d], f_rs.at[d], along(-d))
+        return remote(f_send.at[d], f_recv.at[d], f_ss.at[d], f_rs.at[d], along(home[d]))
 
     def meet(ds):
         first = PLACE[ds[0]] * ROWS
@@ -198,13 +225,11 @@
             )
         for n, d in enumerate(ds):
             part = grad[n * ROWS : (n + 1) * ROWS]
-            if d == 0:
-                own_grad[...] = part
+            if d in (0, 2, 5):
+                keep[PLACE[d]] = part
             else:
                 f_send[d] = part.astype(BF16)
 
-    share.wait_recv()
-    meet((0,))
     to2.wait_recv()
     to1 = pass_text(2, 1, along(-1))
     to3 = pass_text(2, 3, along(1))
@@ -219,9 +244,8 @@
     def _():
         to6.start()
 
-    meet((2, 5))
-    for d in (5, 2):
-        back(d).start()
+    share.wait_recv()
+    meet((0, 2, 5))
     to1.wait_recv()
     to3.wait_recv()
     to4.wait_recv()
@@ -270,23 +294,42 @@
         p_own[v] = p_own[v] + p_recv[v].astype(F32)
         e_send[v] = p_own[v].astype(BF16)
     e_copies = []
-    for j in range(1, NW):
-        copy = remote(e_send.at[lax.rem(w + j, NW)], e_recv.at[j], e_ss.at[j], e_rs.at[j], across(j))
-        copy.start()
-        e_copies.append(copy)
-
-    grad = own_grad[...]
-    for d in (2, 5, 1, 3, 4):
-        back(d).wait_recv()
-        grad = grad + f_recv[d].astype(F32)
-    own_grad[...] = grad
+    for start in (base2, base):
+        for j in (1, 3, 2):
+            n = len(e_copies)
+            copy = remote(
+                e_send.at[start + near(j)], e_recv.at[n], e_ss.at[n], e_rs.at[n], (dp, base + near(j))
+            )
+            copy.start()
+            e_copies.append(copy)
+
+    back(4).wait_recv()
+    keep[PLACE[5]] = keep[PLACE[5]] + f_recv[4].astype(F32)
 
     @pl.when(core == 1)
     def _():
         back(6).wait_recv()
-        own_grad[...] = own_grad[...] + f_recv[6].astype(F32)
-
-    grad = own_grad[...]
+        keep[PLACE[5]] = keep[PLACE[5]] + f_recv[6].astype(F32)
+
+    f_send[5] = keep[PLACE[5]].astype(BF16)
+    back(5).start()
+    back(1).wait_recv()
+    back(3).wait_recv()
+    f_send[2] = (keep[PLACE[2]] + f_recv[1].astype(F32) + f_recv[3].astype(F32)).astype(BF16)
+    back(2).start()
+
+    grad = p_own[w2]
+    for n in range(3):
+        e_copies[n].wait_recv()
+        grad = grad + e_recv[n].astype(F32)
+    z_send[...] = grad.astype(BF16)
+    z_back = remote(z_send, z_recv, z_ss.at[0], z_rs.at[0], partner)
+    z_back.start()
+
+    back(2).wait_recv()
+    grad = keep[PLACE[0]] + f_recv[2].astype(F32)
+    back(5).wait_recv()
+    grad = grad + f_recv[5].astype(F32)
     scaled = unit[...]
     dot = jnp.sum(scaled * grad, axis=1, keepdims=True)
     final = tnorm[:, :1] * (grad - scaled * dot)
@@ -302,9 +345,11 @@
     g_recv[w] = g_send[w]
 
     grad = p_own[w]
-    for j, copy in enumerate(e_copies, 1):
-        copy.wait_recv()
-        grad = grad + e_recv[j].astype(F32)
+    for n in range(3, 6):
+        e_copies[n].wait_recv()
+        grad = grad + e_recv[n].astype(F32)
+    z_back.wait_recv()
+    grad = grad + z_recv[...].astype(F32)
     img_out[...] = grad * inorm
     for copy in g_copies:
         copy.wait_recv()
@@ -312,7 +357,7 @@
 
     for copy in a_copies + b_copies + e_copies + g_copies:
         copy.wait_send()
-    for copy in (to1, to2, to3, to4, to5, share, pair):
+    for copy in (to1, to2, to3, to4, to5, share, pair, z_copy, z_back):
         copy.wait_send()
     for d in range(1, REACH):
         back(d).wait_send()
@@ -350,14 +395,16 @@
                 pltpu.VMEM((ROWS, MAIN), F32),
                 pltpu.VMEM((2, slots * ROWS, COLS), BF16),
                 pltpu.VMEM((2, 8, COLS), F32),
-                pltpu.VMEM((ROWS, D), F32),
                 pltpu.VMEM((slots, ROWS, D), BF16),
                 pltpu.VMEM((slots, ROWS, D), BF16),
                 pltpu.VMEM((NW, FEAT, COLS), BF16),
                 pltpu.VMEM((NW, FEAT, COLS), BF16),
                 pltpu.VMEM((NW, FEAT, COLS), F32),
                 pltpu.VMEM((NW, FEAT, COLS), BF16),
-                pltpu.VMEM((NW, FEAT, COLS), BF16),
+                pltpu.VMEM((6, FEAT, COLS), BF16),
+                pltpu.VMEM((FEAT, COLS), BF16),
+                pltpu.VMEM((FEAT, COLS), BF16),
+                pltpu.VMEM((3, ROWS, D), F32),
                 pltpu.VMEM((NW, ROWS, COLS), F32),
                 pltpu.VMEM((NW, ROWS, COLS), F32),
                 dma((2,)),
@@ -375,9 +422,11 @@
                 dma((NW,)),
                 dma((2,)),
                 dma((2,)),
+                dma((1,)),
+                dma((1,)),
             ],
             compiler_params=pltpu.CompilerParams(
-                collective_id=0, has_side_effects=True, vmem_limit_bytes=40 * 1024 * 1024
+                collective_id=0, has_side_effects=True, vmem_limit_bytes=60 * 1024 * 1024
             ),
         )(image_emb, text_emb, pair_offsets, log_scale, bias)
 

time: 69.7 us -> 63.8 us (0.915)
  the two profiles are of different devices: /device:TPU:56 before, /device:TPU:182 now
where the time goes in v2:
time: 63.8 us; the launch traced here: 63.6 us
  Pallas kernels  59.3 us (93%)
  local copies, waits for them, and re-layouts  2.28 us (4%)
  between operations  1.94 us (3%)
    pallas_call x1, Pallas kernels, body(): pl.pallas_call(functools.partial(kernel, chips), out_shape=(shape, shape)...  59.3 us
    unnamed x4, local copies, waits for them, and re-layouts  2.28 us

profile of v2, /device:TPU:182, one launch (start us, length us, event | category | flops | bytes accessed | tf_op | source)
XLA Modules:
  0.0 63.6 jit_solution(4514354958147483208)
XLA Ops:
  1.9 59.3 %shard_map.68 = (f32[144,256]{1,0:T(8,128)}, f32[144,256]{1,0:T(8,128)}) custom-call(bf16[144,256]{1,0:T(8,128)(2,1)} %img_hbm.1, bf16[144,256]{1,0:T(8,128)(2,1)} %txt_hbm.1, s32[12]{0:T(128)} %offsets.1, f32[1]{0:T(128)S(6)} %copy.9.log_scale, f32[1]{0:T(128)S(6)} %copy.10.bias), custom_call_target="tpu_custom_call" | custom-call | tf_op jit(solution)/shard_map/pallas_call | solution.py:381
  61.3 0.0 copy-start
  61.3 1.6 %copy.11 = f32[144,256]{1,0:T(8,128)} copy(f32[144,256]{1,0:T(8,128)} %get-tuple-element.4) | data formatting | bytes 294912
  62.9 0.0 copy-done
  62.9 0.7 %copy.12 = f32[144,256]{1,0:T(8,128)} copy(f32[144,256]{1,0:T(8,128)S(1)} %copy-done) | data formatting | bytes 294912
Async XLA Ops:
  61.3 1.6 %copy-start = (f32[144,256]{1,0:T(8,128)S(1)}, f32[144,256]{1,0:T(8,128)}, u32[]{:S(2)}) copy-start(f32[144,256]{1,0:T(8,128)} %get-tuple-element.5) | copy-start | bytes 442372

commit v3 on v2

--- a/solution.py
+++ b/solution.py
@@ -128,6 +128,8 @@
     get_img.wait()
     pl.semaphore_wait(barrier, len(peers))
 
+    z_copy = remote(img_raw.at[w], img_raw.at[w], b_ss.at[0], b_rs.at[0], partner)
+    z_copy.start()
     a_copies = []
     for j in range(1, NW):
         copy = remote(a_send.at[lax.rem(w + j, NW)], a_recv.at[w], a_ss.at[j], a_rs.at[j], across(j))
@@ -136,8 +138,6 @@
     a_recv[w] = a_send[w]
     for copy in a_copies:
         copy.wait_recv()
-    z_copy = remote(img_raw.at[w], img_raw.at[w], b_ss.at[0], b_rs.at[0], partner)
-    z_copy.start()
     b_copies = []
     for j in (1, 3, 2):
         copy = remote(img_raw.at[w], img_raw.at[w], b_ss.at[j], b_rs.at[j], (dp, base + near(j)))
@@ -171,6 +171,20 @@
         copy = remote(img_raw.at[w2], img_raw.at[w2], b_ss.at[NX + j], b_rs.at[NX + j], (dp, base + near(j)))
         copy.start()
         b_copies.append(copy)
+
+    to2.wait_recv()
+    to1 = pass_text(2, 1, along(-1))
+    to3 = pass_text(2, 3, along(1))
+    to1.start()
+    to3.start()
+    to5.wait_recv()
+    to4 = pass_text(5, 4, along(-1))
+    to6 = pass_text(5, 6, along(1))
+    to4.start()
+
+    @pl.when(core == 1)
+    def _():
+        to6.start()
 
     def squares(v):
         return jnp.sum(jnp.square(img_raw[v].astype(F32)), axis=0, keepdims=True)
@@ -229,20 +243,6 @@
                 keep[PLACE[d]] = part
             else:
                 f_send[d] = part.astype(BF16)
-
-    to2.wait_recv()
-    to1 = pass_text(2, 1, along(-1))
-    to3 = pass_text(2, 3, along(1))
-    to1.start()
-    to3.start()
-    to5.wait_recv()
-    to4 = pass_text(5, 4, along(-1))
-    to6 = pass_text(5, 6, along(1))
-    to4.start()
-
-    @pl.when(core == 1)
-    def _():
-        to6.start()
 
     share.wait_recv()
     meet((0, 2, 5))

time: 63.8 us -> 60.8 us (0.953)
  the two profiles are of different devices: /device:TPU:182 before, /device:TPU:48 now
where the time goes in v3:
time: 60.8 us; the launch traced here: 60.6 us
  Pallas kernels  56.4 us (93%)
  local copies, waits for them, and re-layouts  2.28 us (4%)
  between operations  1.94 us (3%)
    pallas_call x1, Pallas kernels, body(): pl.pallas_call(functools.partial(kernel, chips), out_shape=(shape, shape)...  56.4 us
    unnamed x4, local copies, waits for them, and re-layouts  2.28 us

profile of v3, /device:TPU:48, one launch (start us, length us, event | category | flops | bytes accessed | tf_op | source)
XLA Modules:
  0.0 60.6 jit_solution(6442934449147889789)
XLA Ops:
  1.9 56.4 %shard_map.68 = (f32[144,256]{1,0:T(8,128)}, f32[144,256]{1,0:T(8,128)}) custom-call(bf16[144,256]{1,0:T(8,128)(2,1)} %img_hbm.1, bf16[144,256]{1,0:T(8,128)(2,1)} %txt_hbm.1, s32[12]{0:T(128)} %offsets.1, f32[1]{0:T(128)S(6)} %copy.9.log_scale, f32[1]{0:T(128)S(6)} %copy.10.bias), custom_call_target="tpu_custom_call" | custom-call | tf_op jit(solution)/shard_map/pallas_call | solution.py:381
  58.3 0.0 copy-start
  58.3 1.6 %copy.11 = f32[144,256]{1,0:T(8,128)} copy(f32[144,256]{1,0:T(8,128)} %get-tuple-element.4) | data formatting | bytes 294912
  60.0 0.0 copy-done
  60.0 0.7 %copy.12 = f32[144,256]{1,0:T(8,128)} copy(f32[144,256]{1,0:T(8,128)S(1)} %copy-done) | data formatting | bytes 294912
Async XLA Ops:
  58.3 1.6 %copy-start = (f32[144,256]{1,0:T(8,128)S(1)}, f32[144,256]{1,0:T(8,128)}, u32[]{:S(2)}) copy-start(f32[144,256]{1,0:T(8,128)} %get-tuple-element.5) | copy-start | bytes 442372

commit v4 on v3

--- a/solution.py
+++ b/solution.py
@@ -33,11 +33,13 @@
     chips,
     img_hbm,
     txt_hbm,
+    offsets_hbm,
+    scale_hbm,
+    bias_hbm,
+    out_hbm,
     offsets,
     log_scale,
     bias,
-    img_out,
-    txt_out,
     img_raw,
     txt_in,
     txt_wide,
@@ -61,6 +63,9 @@
     keep,
     g_send,
     g_recv,
+    h_send,
+    h_recv,
+    out,
     local_sem,
     a_ss,
     a_rs,
@@ -78,6 +83,8 @@
     s_rs,
     z_ss,
     z_rs,
+    h_ss,
+    h_rs,
 ):
     dp = lax.axis_index("dp")
     w = lax.axis_index("width")
@@ -106,8 +113,7 @@
         )
 
     barrier = pltpu.get_barrier_semaphore()
-    peers = [across(j) for j in range(1, NW)] + [other]
-    peers += [along(d) for d in range(-REACH, REACH + 1) if d != 0]
+    peers = [along(d) for d in (5, -5, 2, -2, 1, -1)] + [across(j) for j in range(1, NW)] + [other]
     for peer in peers:
         pl.semaphore_signal(barrier, inc=1, device_id=peer, device_id_type=MESH)
 
@@ -115,6 +121,12 @@
     get_img = pltpu.make_async_copy(img_hbm, img_raw.at[w], local_sem.at[1])
     get_txt.start()
     get_img.start()
+    scalars = [
+        pltpu.make_async_copy(src, dst, local_sem.at[2 + n])
+        for n, (src, dst) in enumerate(((offsets_hbm, offsets), (scale_hbm, log_scale), (bias_hbm, bias)))
+    ]
+    for copy in scalars:
+        copy.start()
 
     @pl.when(core == 0)
     def _():
@@ -126,6 +138,8 @@
     txt_wide[:FEAT, :] = txt_in[...].astype(F32)
     a_send[...] = txt_wide[...].T.astype(BF16).reshape(NW, ROWS, COLS)
     get_img.wait()
+    for copy in scalars:
+        copy.wait()
     pl.semaphore_wait(barrier, len(peers))
 
     z_copy = remote(img_raw.at[w], img_raw.at[w], b_ss.at[0], b_rs.at[0], partner)
@@ -208,7 +222,7 @@
     row = lax.broadcasted_iota(jnp.int32, (ROWS, COLS), 0) + w * ROWS
     gap = col - row
 
-    home = {1: 1, 3: -1, 4: 1, 6: -1, 2: -2, 5: -5}
+    home = {1: 1, 3: -1, 4: 1, 6: -1}
 
     def back(d):
         return remote(f_send.at[d], f_recv.at[d], f_ss.at[d], f_rs.at[d], along(home[d]))
@@ -303,6 +317,47 @@
             copy.start()
             e_copies.append(copy)
 
+    lane = lax.broadcasted_iota(jnp.int32, (ROWS, MAIN), 1)
+
+    def pieces(part, fill, store):
+        tail = part[:, NW * MAIN :]
+        for v in range(NW):
+            rest = pltpu.roll(tail, MAIN - v * TAIL, 1) if v else tail
+            store(v, part[:, v * MAIN : (v + 1) * MAIN], jnp.where(lane < TAIL, rest, fill))
+
+    def to_row(v, main, rest):
+        g_send[v, :, :MAIN] = main
+        g_send[v, :, MAIN:] = rest
+
+    scaled = unit[...]
+    part = keep[PLACE[0]]
+    part = part - scaled * jnp.sum(scaled * part, axis=1, keepdims=True)
+    pieces(part, tnorm[...], to_row)
+    g_copies = []
+    for j in range(1, NW):
+        copy = remote(g_send.at[lax.rem(w + j, NW)], g_recv.at[w], g_ss.at[j], g_rs.at[j], across(j))
+        copy.start()
+        g_copies.append(copy)
+    g_recv[w] = g_send[w]
+
+    h_copies = []
+
+    def send_home(t, d, part):
+        text = txt[rows_of(d), :].astype(F32)
+        part = part - text * jnp.sum(text * part, axis=1, keepdims=True)
+
+        def to_home(v, main, rest):
+            h_send[t, v, :, :MAIN] = main.astype(BF16)
+            h_send[t, v, :, MAIN:] = rest.astype(BF16)
+
+        pieces(part, 0.0, to_home)
+        owner = lax.rem(chip - d + chips, chips) * 2 + core
+        for j in range(NW):
+            to = lax.rem(w + j, NW)
+            copy = remote(h_send.at[t, to], h_recv.at[t, w], h_ss.at[t, j], h_rs.at[t, j], (owner, to))
+            copy.start()
+            h_copies.append(copy)
+
     back(4).wait_recv()
     keep[PLACE[5]] = keep[PLACE[5]] + f_recv[4].astype(F32)
 
@@ -311,12 +366,10 @@
         back(6).wait_recv()
         keep[PLACE[5]] = keep[PLACE[5]] + f_recv[6].astype(F32)
 
-    f_send[5] = keep[PLACE[5]].astype(BF16)
-    back(5).start()
+    send_home(0, 5, keep[PLACE[5]])
     back(1).wait_recv()
     back(3).wait_recv()
-    f_send[2] = (keep[PLACE[2]] + f_recv[1].astype(F32) + f_recv[3].astype(F32)).astype(BF16)
-    back(2).start()
+    send_home(1, 2, keep[PLACE[2]] + f_recv[1].astype(F32) + f_recv[3].astype(F32))
 
     grad = p_own[w2]
     for n in range(3):
@@ -326,46 +379,37 @@
     z_back = remote(z_send, z_recv, z_ss.at[0], z_rs.at[0], partner)
     z_back.start()
 
-    back(2).wait_recv()
-    grad = keep[PLACE[0]] + f_recv[2].astype(F32)
-    back(5).wait_recv()
-    grad = grad + f_recv[5].astype(F32)
-    scaled = unit[...]
-    dot = jnp.sum(scaled * grad, axis=1, keepdims=True)
-    final = tnorm[:, :1] * (grad - scaled * dot)
-    tail = final[:, NW * MAIN :]
-    for v in range(NW):
-        g_send[v, :, :MAIN] = final[:, v * MAIN : (v + 1) * MAIN]
-        g_send[v, :, MAIN:] = pltpu.roll(tail, MAIN - v * TAIL, 1) if v else tail
-    g_copies = []
-    for j in range(1, NW):
-        copy = remote(g_send.at[lax.rem(w + j, NW)], g_recv.at[w], g_ss.at[j], g_rs.at[j], across(j))
-        copy.start()
-        g_copies.append(copy)
-    g_recv[w] = g_send[w]
-
     grad = p_own[w]
     for n in range(3, 6):
         e_copies[n].wait_recv()
         grad = grad + e_recv[n].astype(F32)
     z_back.wait_recv()
     grad = grad + z_recv[...].astype(F32)
-    img_out[...] = grad * inorm
-    for copy in g_copies:
+    out[0] = grad * inorm
+    put_img = pltpu.make_async_copy(out.at[0], out_hbm.at[pl.ds(0, FEAT), :], local_sem.at[5])
+    put_img.start()
+    for copy in g_copies + h_copies:
         copy.wait_recv()
-    txt_out[...] = g_recv[...].reshape(COLS, COLS).T[:FEAT]
-
-    for copy in a_copies + b_copies + e_copies + g_copies:
+    whole = g_recv[...] + h_recv[0].astype(F32) + h_recv[1].astype(F32)
+    whole = whole.reshape(COLS, COLS).T
+    out[1] = whole[:FEAT] * whole[FEAT : FEAT + 1]
+    put_txt = pltpu.make_async_copy(out.at[1], out_hbm.at[pl.ds(FEAT, FEAT), :], local_sem.at[6])
+    put_txt.start()
+
+    for copy in a_copies + b_copies + e_copies + g_copies + h_copies:
         copy.wait_send()
     for copy in (to1, to2, to3, to4, to5, share, pair, z_copy, z_back):
         copy.wait_send()
-    for d in range(1, REACH):
+    for d in (1, 3, 4):
         back(d).wait_send()
 
     @pl.when(core == 1)
     def _():
         to6.wait_send()
         back(6).wait_send()
+
+    put_img.wait()
+    put_txt.wait()
 
 
 def solution(mesh):
@@ -374,16 +418,17 @@
     dma = pltpu.SemaphoreType.DMA
 
     def body(image_emb, text_emb, pair_offsets, log_scale, bias):
-        shape = jax.ShapeDtypeStruct((FEAT, COLS), F32)
-        any_space = pl.BlockSpec(memory_space=pl.ANY)
-        smem = pl.BlockSpec(memory_space=pltpu.SMEM)
-        vmem = pl.BlockSpec(memory_space=pltpu.VMEM)
-        return pl.pallas_call(
+        shape = jax.ShapeDtypeStruct((2 * FEAT, COLS), F32)
+        hbm = pl.BlockSpec(memory_space=pltpu.HBM)
+        grads = pl.pallas_call(
             functools.partial(kernel, chips),
-            out_shape=(shape, shape),
-            in_specs=[any_space, any_space, smem, smem, smem],
-            out_specs=(vmem, vmem),
+            out_shape=shape,
+            in_specs=[hbm] * 5,
+            out_specs=hbm,
             scratch_shapes=[
+                pltpu.SMEM((CYCLE,), jnp.int32),
+                pltpu.SMEM((1,), F32),
+                pltpu.SMEM((1,), F32),
                 pltpu.VMEM((NW, FEAT, COLS), BF16),
                 pltpu.VMEM((FEAT, COLS), BF16),
                 pltpu.VMEM((COLS, COLS), F32),
@@ -407,7 +452,10 @@
                 pltpu.VMEM((3, ROWS, D), F32),
                 pltpu.VMEM((NW, ROWS, COLS), F32),
                 pltpu.VMEM((NW, ROWS, COLS), F32),
-                dma((2,)),
+                pltpu.VMEM((2, NW, ROWS, COLS), BF16),
+                pltpu.VMEM((2, NW, ROWS, COLS), BF16),
+                pltpu.VMEM((2, FEAT, COLS), F32),
+                dma((7,)),
                 dma((NW,)),
                 dma((NW,)),
                 dma((NW,)),
@@ -424,11 +472,14 @@
                 dma((2,)),
                 dma((1,)),
                 dma((1,)),
+                dma((2, NW)),
+                dma((2, NW)),
             ],
             compiler_params=pltpu.CompilerParams(
                 collective_id=0, has_side_effects=True, vmem_limit_bytes=60 * 1024 * 1024
             ),
         )(image_emb, text_emb, pair_offsets, log_scale, bias)
+        return grads[:FEAT], grads[FEAT:]
 
     placed = (P("width", "dp"), P("width", "dp"), P(), P(), P())
     return jax.shard_map(

time: 60.8 us -> 59.2 us (0.974)
  the two profiles are of different devices: /device:TPU:48 before, /device:TPU:57 now
where the time goes in v4:
time: 59.2 us; the launch traced here: 59 us
  Pallas kernels  55.4 us (94%)
  between operations  1.93 us (3%)
  local copies, waits for them, and re-layouts  1.71 us (3%)
    pallas_call x1, Pallas kernels, body(): pl.pallas_call(functools.partial(kernel, chips), out_shape=shape, in_spec...  55.4 us
    slice x1, local copies, waits for them, and re-layouts, body(): return (grads[:FEAT], grads[FEAT:])  1.71 us

profile of v4, /device:TPU:57, one launch (start us, length us, event | category | flops | bytes accessed | tf_op | source)
XLA Modules:
  0.0 59.0 jit_solution(6402267058491402984)
XLA Ops:
  1.9 55.4 %shard_map.68 = f32[288,256]{1,0:T(8,128)} custom-call(bf16[144,256]{1,0:T(8,128)(2,1)} %img_hbm.1, bf16[144,256]{1,0:T(8,128)(2,1)} %txt_hbm.1, s32[12]{0:T(128)} %offsets_hbm.1, f32[1]{0:T(128)S(6)} %copy.7.scale_hbm, f32[1]{0:T(128)S(6)} %copy.8.bias_hbm), custom_call_target="tpu_custom_call" | custom-call | tf_op jit(solution)/shard_map/pallas_call | solution.py:423
  57.3 1.7 %fusion = (f32[144,256]{1,0:T(8,128)}, f32[144,256]{1,0:T(8,128)}) fusion(f32[288,256]{1,0:T(8,128)} %shard_map.68), kind=kLoop, calls=%fused_computation | loop fusion | bytes 589824 | tf_op jit(solution)/shard_map/slice | solution.py:482

commit v5 on v4

--- a/solution.py
+++ b/solution.py
@@ -20,6 +20,7 @@
 D = NW * FEAT
 COLS = 256
 ROWS = COLS // NW
+NY = 8
 REACH = 6
 ORDER = (0, 2, 5, 1, 3, 4, 6)
 PLACE = {d: i for i, d in enumerate(ORDER)}
@@ -34,12 +35,10 @@
     img_hbm,
     txt_hbm,
     offsets_hbm,
-    scale_hbm,
-    bias_hbm,
-    out_hbm,
-    offsets,
     log_scale,
     bias,
+    out,
+    offsets,
     img_raw,
     txt_in,
     txt_wide,
@@ -65,7 +64,6 @@
     g_recv,
     h_send,
     h_recv,
-    out,
     local_sem,
     a_ss,
     a_rs,
@@ -98,6 +96,8 @@
         return (dp, lax.rem(w + j, NW))
 
     other = (dp + 1 - 2 * core, w)
+    y = lax.rem(chip, NY)
+    first, last = y == 0, y == NY - 1
     x = lax.rem(w, NX)
     base = w - x
     base2 = NX - base
@@ -121,12 +121,8 @@
     get_img = pltpu.make_async_copy(img_hbm, img_raw.at[w], local_sem.at[1])
     get_txt.start()
     get_img.start()
-    scalars = [
-        pltpu.make_async_copy(src, dst, local_sem.at[2 + n])
-        for n, (src, dst) in enumerate(((offsets_hbm, offsets), (scale_hbm, log_scale), (bias_hbm, bias)))
-    ]
-    for copy in scalars:
-        copy.start()
+    get_offsets = pltpu.make_async_copy(offsets_hbm, offsets, local_sem.at[2])
+    get_offsets.start()
 
     @pl.when(core == 0)
     def _():
@@ -138,8 +134,7 @@
     txt_wide[:FEAT, :] = txt_in[...].astype(F32)
     a_send[...] = txt_wide[...].T.astype(BF16).reshape(NW, ROWS, COLS)
     get_img.wait()
-    for copy in scalars:
-        copy.wait()
+    get_offsets.wait()
     pl.semaphore_wait(barrier, len(peers))
 
     z_copy = remote(img_raw.at[w], img_raw.at[w], b_ss.at[0], b_rs.at[0], partner)
@@ -172,13 +167,22 @@
     tnorm[...] = jnp.broadcast_to(norm, tnorm.shape)
     txt[rows_of(0), :] = scaled.astype(BF16)
 
-    def pass_text(src, dst, to):
-        return remote(txt.at[rows_of(src)], txt.at[rows_of(dst)], c_ss.at[dst], c_rs.at[dst], to)
+    def pass_text(src, dst, to, sem=None):
+        sem = dst if sem is None else sem
+        return remote(txt.at[rows_of(src)], txt.at[rows_of(dst)], c_ss.at[sem], c_rs.at[dst], to)
 
     to2 = pass_text(0, 2, along(2))
     to5 = pass_text(0, 5, along(5))
     to5.start()
     to2.start()
+    to1_last = pass_text(0, 1, along(1), 0)
+    to4_last = pass_text(2, 4, along(2), 0)
+    to3_first = pass_text(5, 3, along(-2), 0)
+
+    @pl.when(y == NY - 2)
+    def _():
+        to1_last.start()
+
 
     z_copy.wait_recv()
     for j in (1, 3, 2):
@@ -189,16 +193,34 @@
     to2.wait_recv()
     to1 = pass_text(2, 1, along(-1))
     to3 = pass_text(2, 3, along(1))
-    to1.start()
-    to3.start()
+
+    @pl.when(y != 0)
+    def _():
+        to1.start()
+
+    @pl.when(y != NY - 1)
+    def _():
+        to3.start()
+
+    @pl.when(y == NY - 3)
+    def _():
+        to4_last.start()
+
     to5.wait_recv()
     to4 = pass_text(5, 4, along(-1))
     to6 = pass_text(5, 6, along(1))
-    to4.start()
+
+    @pl.when(y != 0)
+    def _():
+        to4.start()
 
     @pl.when(core == 1)
     def _():
         to6.start()
+
+    @pl.when(y == 2)
+    def _():
+        to3_first.start()
 
     def squares(v):
         return jnp.sum(jnp.square(img_raw[v].astype(F32)), axis=0, keepdims=True)
@@ -222,10 +244,20 @@
     row = lax.broadcasted_iota(jnp.int32, (ROWS, COLS), 0) + w * ROWS
     gap = col - row
 
-    home = {1: 1, 3: -1, 4: 1, 6: -1}
+    home = {
+        1: (jnp.where(last, -1, 1), jnp.where(last, 0, 1)),
+        3: (jnp.where(first, 2, -1), jnp.where(first, 5, 3)),
+        4: (jnp.where(last, -2, 1), jnp.where(last, 2, 4)),
+        6: (-1, 6),
+    }
 
     def back(d):
-        return remote(f_send.at[d], f_recv.at[d], f_ss.at[d], f_rs.at[d], along(home[d]))
+        to, slot = home[d]
+        return remote(f_send.at[d], f_recv.at[slot], f_ss.at[d], f_rs.at[slot], along(to))
+
+    def add_part(place, slot):
+        remote(f_send.at[slot], f_recv.at[slot], f_ss.at[slot], f_rs.at[slot], other).wait_recv()
+        keep[place] = keep[place] + f_recv[slot].astype(F32)
 
     def meet(ds):
         first = PLACE[ds[0]] * ROWS
@@ -329,6 +361,56 @@
         g_send[v, :, :MAIN] = main
         g_send[v, :, MAIN:] = rest
 
+    h_copies = []
+
+    def send_home(t, d, part):
+        text = txt[rows_of(d), :].astype(F32)
+        part = part - text * jnp.sum(text * part, axis=1, keepdims=True)
+
+        def to_home(v, main, rest):
+            h_send[t, v, :, :MAIN] = main.astype(BF16)
+            h_send[t, v, :, MAIN:] = rest.astype(BF16)
+
+        pieces(part, 0.0, to_home)
+        owner = lax.rem(chip - d + chips, chips) * 2 + core
+        for j in range(NW):
+            to = lax.rem(w + j, NW)
+            copy = remote(h_send.at[t, to], h_recv.at[t, w], h_ss.at[t, j], h_rs.at[t, j], (owner, to))
+            copy.start()
+            h_copies.append(copy)
+
+    @pl.when(y != 0)
+    def _():
+        add_part(PLACE[5], 4)
+
+    @pl.when(core == 1)
+    def _():
+        add_part(PLACE[5], 6)
+
+    @pl.when(y == 2)
+    def _():
+        add_part(PLACE[5], 5)
+
+    send_home(0, 5, keep[PLACE[5]])
+
+    @pl.when(y != 0)
+    def _():
+        add_part(PLACE[2], 1)
+
+    @pl.when(y != NY - 1)
+    def _():
+        add_part(PLACE[2], 3)
+
+    @pl.when(y == NY - 3)
+    def _():
+        add_part(PLACE[2], 2)
+
+    send_home(1, 2, keep[PLACE[2]])
+
+    @pl.when(y == NY - 2)
+    def _():
+        add_part(PLACE[0], 0)
+
     scaled = unit[...]
     part = keep[PLACE[0]]
     part = part - scaled * jnp.sum(scaled * part, axis=1, keepdims=True)
@@ -340,37 +422,6 @@
         g_copies.append(copy)
     g_recv[w] = g_send[w]
 
-    h_copies = []
-
-    def send_home(t, d, part):
-        text = txt[rows_of(d), :].astype(F32)
-        part = part - text * jnp.sum(text * part, axis=1, keepdims=True)
-
-        def to_home(v, main, rest):
-            h_send[t, v, :, :MAIN] = main.astype(BF16)
-            h_send[t, v, :, MAIN:] = rest.astype(BF16)
-
-        pieces(part, 0.0, to_home)
-        owner = lax.rem(chip - d + chips, chips) * 2 + core
-        for j in range(NW):
-            to = lax.rem(w + j, NW)
-            copy = remote(h_send.at[t, to], h_recv.at[t, w], h_ss.at[t, j], h_rs.at[t, j], (owner, to))
-            copy.start()
-            h_copies.append(copy)
-
-    back(4).wait_recv()
-    keep[PLACE[5]] = keep[PLACE[5]] + f_recv[4].astype(F32)
-
-    @pl.when(core == 1)
-    def _():
-        back(6).wait_recv()
-        keep[PLACE[5]] = keep[PLACE[5]] + f_recv[6].astype(F32)
-
-    send_home(0, 5, keep[PLACE[5]])
-    back(1).wait_recv()
-    back(3).wait_recv()
-    send_home(1, 2, keep[PLACE[2]] + f_recv[1].astype(F32) + f_recv[3].astype(F32))
-
     grad = p_own[w2]
     for n in range(3):
         e_copies[n].wait_recv()
@@ -385,31 +436,34 @@
         grad = grad + e_recv[n].astype(F32)
     z_back.wait_recv()
     grad = grad + z_recv[...].astype(F32)
-    out[0] = grad * inorm
-    put_img = pltpu.make_async_copy(out.at[0], out_hbm.at[pl.ds(0, FEAT), :], local_sem.at[5])
-    put_img.start()
+    out[:FEAT] = grad * inorm
     for copy in g_copies + h_copies:
         copy.wait_recv()
     whole = g_recv[...] + h_recv[0].astype(F32) + h_recv[1].astype(F32)
     whole = whole.reshape(COLS, COLS).T
-    out[1] = whole[:FEAT] * whole[FEAT : FEAT + 1]
-    put_txt = pltpu.make_async_copy(out.at[1], out_hbm.at[pl.ds(FEAT, FEAT), :], local_sem.at[6])
-    put_txt.start()
+    out[FEAT:] = whole[:FEAT] * whole[FEAT : FEAT + 1]
 
     for copy in a_copies + b_copies + e_copies + g_copies + h_copies:
         copy.wait_send()
-    for copy in (to1, to2, to3, to4, to5, share, pair, z_copy, z_back):
+    for copy in (to2, to5, share, pair, z_copy, z_back):
         copy.wait_send()
     for d in (1, 3, 4):
         back(d).wait_send()
 
+    for here, copy in (
+        (y != 0, to1),
+        (y != NY - 1, to3),
+        (y != 0, to4),
+        (y == NY - 2, to1_last),
+        (y == NY - 3, to4_last),
+        (y == 2, to3_first),
+    ):
+        pl.when(here)(copy.wait_send)
+
     @pl.when(core == 1)
     def _():
         to6.wait_send()
         back(6).wait_send()
-
-    put_img.wait()
-    put_txt.wait()
 
 
 def solution(mesh):
@@ -419,16 +473,15 @@
 
     def body(image_emb, text_emb, pair_offsets, log_scale, bias):
         shape = jax.ShapeDtypeStruct((2 * FEAT, COLS), F32)
+        smem = pl.BlockSpec(memory_space=pltpu.SMEM)
         hbm = pl.BlockSpec(memory_space=pltpu.HBM)
         grads = pl.pallas_call(
             functools.partial(kernel, chips),
             out_shape=shape,
-            in_specs=[hbm] * 5,
-            out_specs=hbm,
+            in_specs=[hbm, hbm, hbm, smem, smem],
+            out_specs=pl.BlockSpec(memory_space=pltpu.VMEM),
             scratch_shapes=[
                 pltpu.SMEM((CYCLE,), jnp.int32),
-                pltpu.SMEM((1,), F32),
-                pltpu.SMEM((1,), F32),
                 pltpu.VMEM((NW, FEAT, COLS), BF16),
                 pltpu.VMEM((FEAT, COLS), BF16),
                 pltpu.VMEM((COLS, COLS), F32),
@@ -454,8 +507,7 @@
                 pltpu.VMEM((NW, ROWS, COLS), F32),
                 pltpu.VMEM((2, NW, ROWS, COLS), BF16),
                 pltpu.VMEM((2, NW, ROWS, COLS), BF16),
-                pltpu.VMEM((2, FEAT, COLS), F32),
-                dma((7,)),
+                dma((3,)),
                 dma((NW,)),
                 dma((NW,)),
                 dma((NW,)),
@@ -476,9 +528,11 @@
                 dma((2, NW)),
             ],
             compiler_params=pltpu.CompilerParams(
-                collective_id=0, has_side_effects=True, vmem_limit_bytes=60 * 1024 * 1024
+                collective_id=0, has_side_effects=True, vmem_limit_bytes=40 * 1024 * 1024
             ),
-        )(image_emb, text_emb, pair_offsets, log_scale, bias)
+        )(
+            *(pltpu.with_memory_space_constraint(v, pltpu.HBM) for v in (image_emb, text_emb, pair_offsets)), log_scale, bias
+        )
         return grads[:FEAT], grads[FEAT:]
 
     placed = (P("width", "dp"), P("width", "dp"), P(), P(), P())

time: 59.2 us -> 56.7 us (0.958)
  Pallas kernels: 55.4 us -> 53.9 us
  local copies, waits for them, and re-layouts: 1.71 us -> 0.73 us
    pallas_call x1, Pallas kernels: 55.4 us -> 53.9 us  [body(): pl.pallas_call(functools.partial(kernel, chips), out_shape=shape, in_spec...]
    slice x1, local copies, waits for them, and re-layouts: 1.71 us -> 0.73 us  [body(): return (grads[:FEAT], grads[FEAT:])]
where the time goes in v5:
time: 56.7 us; the launch traced here: 56.5 us
  Pallas kernels  53.9 us (95%)
  between operations  1.93 us (3%)
  local copies, waits for them, and re-layouts  0.73 us (1%)
    pallas_call x1, Pallas kernels, body(): pl.pallas_call(functools.partial(kernel, chips), out_shape=shape, in_spec...  53.9 us

profile of v5, /device:TPU:57, one launch (start us, length us, event | category | flops | bytes accessed | tf_op | source)
XLA Modules:
  0.0 56.5 jit_solution(5363047649500322827)
XLA Ops:
  1.9 53.9 %shard_map.68 = f32[288,256]{1,0:T(8,128)S(1)} custom-call(bf16[144,256]{1,0:T(8,128)(2,1)} %img_hbm.1, bf16[144,256]{1,0:T(8,128)(2,1)} %txt_hbm.1, s32[12]{0:T(128)} %offsets_hbm.1, f32[1]{0:T(128)S(6)} %copy.7.log_scale, f32[1]{0:T(128)S(6)} %copy.8.bias), custom_call_target="tpu_custom_call" | custom-call | tf_op jit(solution)/shard_map/pallas_call | solution.py:478
  55.8 0.7 %fusion = (f32[144,256]{1,0:T(8,128)}, f32[144,256]{1,0:T(8,128)}) fusion(f32[288,256]{1,0:T(8,128)S(1)} %shard_map.68), kind=kLoop, calls=%fused_computation | loop fusion | bytes 589824 | tf_op jit(solution)/shard_map/slice | solution.py:536

commit v6 on v5

--- a/solution.py
+++ b/solution.py
@@ -335,31 +335,57 @@
     pair = remote(p_send, p_recv, s_ss.at[1], s_rs.at[1], other)
     pair.start()
     image_part(core, to_own)
+
+    lane = lax.broadcasted_iota(jnp.int32, (8, MAIN), 1)
+
+    def pieces(part, more, store):
+        tail = part[:, NW * MAIN :]
+        for v in range(NW):
+            packed = more
+            for q in range(4):
+                shift = (32 * q - v * TAIL) % MAIN
+                rest = tail[8 * q : 8 * q + 8]
+                rest = pltpu.roll(rest, shift, 1) if shift else rest
+                packed = jnp.where((lane >= 32 * q) & (lane < 32 * q + TAIL), rest, packed)
+            rest = jnp.concatenate([packed, jnp.zeros((8, MAIN), F32)], axis=0)
+            store(v, part[:, v * MAIN : (v + 1) * MAIN].astype(BF16), rest.astype(BF16))
+
+    def to_row(v, main, rest):
+        g_send[v, :ROWS, :] = main
+        g_send[v, ROWS:, :] = rest
+
+    g_copies = [
+        remote(g_send.at[lax.rem(w + j, NW)], g_recv.at[w], g_ss.at[j], g_rs.at[j], across(j)) for j in range(1, NW)
+    ]
+
+    def send_own():
+        scaled = unit[...]
+        part = keep[PLACE[0]]
+        part = part - scaled * jnp.sum(scaled * part, axis=1, keepdims=True)
+        norm = tnorm[...]
+        high = norm.astype(BF16).astype(F32)
+        norms = jnp.zeros((8, MAIN), F32)
+        for q in range(4):
+            norms = jnp.where(lane == 32 * q + TAIL, high[8 * q : 8 * q + 8], norms)
+            norms = jnp.where(lane == 32 * q + TAIL + 1, (norm - high)[8 * q : 8 * q + 8], norms)
+        pieces(part, norms, to_row)
+        for copy in g_copies:
+            copy.start()
+        g_recv[w] = g_send[w]
+
+    pl.when(y != NY - 2)(send_own)
+
     pair.wait_recv()
     for v in range(NW):
         p_own[v] = p_own[v] + p_recv[v].astype(F32)
         e_send[v] = p_own[v].astype(BF16)
-    e_copies = []
-    for start in (base2, base):
-        for j in (1, 3, 2):
-            n = len(e_copies)
-            copy = remote(
-                e_send.at[start + near(j)], e_recv.at[n], e_ss.at[n], e_rs.at[n], (dp, base + near(j))
-            )
-            copy.start()
-            e_copies.append(copy)
-
-    lane = lax.broadcasted_iota(jnp.int32, (ROWS, MAIN), 1)
-
-    def pieces(part, fill, store):
-        tail = part[:, NW * MAIN :]
-        for v in range(NW):
-            rest = pltpu.roll(tail, MAIN - v * TAIL, 1) if v else tail
-            store(v, part[:, v * MAIN : (v + 1) * MAIN], jnp.where(lane < TAIL, rest, fill))
-
-    def to_row(v, main, rest):
-        g_send[v, :, :MAIN] = main
-        g_send[v, :, MAIN:] = rest
+    e_copies = [
+        remote(e_send.at[start + near(j)], e_recv.at[n + j], e_ss.at[n + j], e_rs.at[n + j], (dp, base + near(j)))
+        for n, start in ((NX, base2), (0, base))
+        for j in (1, 3, 2)
+    ]
+    for copy in e_copies[:3]:
+        copy.start()
 
     h_copies = []
 
@@ -368,10 +394,10 @@
         part = part - text * jnp.sum(text * part, axis=1, keepdims=True)
 
         def to_home(v, main, rest):
-            h_send[t, v, :, :MAIN] = main.astype(BF16)
-            h_send[t, v, :, MAIN:] = rest.astype(BF16)
-
-        pieces(part, 0.0, to_home)
+            h_send[t, v, :ROWS, :] = main
+            h_send[t, v, ROWS:, :] = rest
+
+        pieces(part, jnp.zeros((8, MAIN), F32), to_home)
         owner = lax.rem(chip - d + chips, chips) * 2 + core
         for j in range(NW):
             to = lax.rem(w + j, NW)
@@ -410,38 +436,36 @@
     @pl.when(y == NY - 2)
     def _():
         add_part(PLACE[0], 0)
-
-    scaled = unit[...]
-    part = keep[PLACE[0]]
-    part = part - scaled * jnp.sum(scaled * part, axis=1, keepdims=True)
-    pieces(part, tnorm[...], to_row)
-    g_copies = []
-    for j in range(1, NW):
-        copy = remote(g_send.at[lax.rem(w + j, NW)], g_recv.at[w], g_ss.at[j], g_rs.at[j], across(j))
-        copy.start()
-        g_copies.append(copy)
-    g_recv[w] = g_send[w]
+        send_own()
 
     grad = p_own[w2]
-    for n in range(3):
-        e_copies[n].wait_recv()
-        grad = grad + e_recv[n].astype(F32)
+    for j, copy in zip((1, 3, 2), e_copies[:3]):
+        copy.wait_recv()
+        grad = grad + e_recv[NX + j].astype(F32)
     z_send[...] = grad.astype(BF16)
     z_back = remote(z_send, z_recv, z_ss.at[0], z_rs.at[0], partner)
     z_back.start()
-
+    for copy in e_copies[3:]:
+        copy.start()
     grad = p_own[w]
-    for n in range(3, 6):
-        e_copies[n].wait_recv()
-        grad = grad + e_recv[n].astype(F32)
+    for j, copy in zip((1, 3, 2), e_copies[3:]):
+        copy.wait_recv()
+        grad = grad + e_recv[j].astype(F32)
     z_back.wait_recv()
     grad = grad + z_recv[...].astype(F32)
     out[:FEAT] = grad * inorm
     for copy in g_copies + h_copies:
         copy.wait_recv()
-    whole = g_recv[...] + h_recv[0].astype(F32) + h_recv[1].astype(F32)
-    whole = whole.reshape(COLS, COLS).T
-    out[FEAT:] = whole[:FEAT] * whole[FEAT : FEAT + 1]
+    whole = g_recv[...].astype(F32) + h_recv[0].astype(F32) + h_recv[1].astype(F32)
+    txt_wide[:, :MAIN] = whole[:, :ROWS].reshape(COLS, MAIN)
+    packed = whole[:, ROWS : ROWS + 8].reshape(NW * 8, MAIN)
+    for q in range(4):
+        rest = pltpu.roll(packed, MAIN - 32 * q, 1) if q else packed
+        for v in range(NW):
+            at = v * ROWS + 8 * q
+            txt_wide[at : at + 8, MAIN:] = rest[8 * v : 8 * v + 8]
+    whole = txt_wide[...].T
+    out[FEAT:] = whole[:FEAT] * (whole[FEAT : FEAT + 1] + whole[FEAT + 1 : FEAT + 2])
 
     for copy in a_copies + b_copies + e_copies + g_copies + h_copies:
         copy.wait_send()
@@ -499,14 +523,14 @@
                 pltpu.VMEM((NW, FEAT, COLS), BF16),
                 pltpu.VMEM((NW, FEAT, COLS), F32),
                 pltpu.VMEM((NW, FEAT, COLS), BF16),
-                pltpu.VMEM((6, FEAT, COLS), BF16),
+                pltpu.VMEM((NW, FEAT, COLS), BF16),
                 pltpu.VMEM((FEAT, COLS), BF16),
                 pltpu.VMEM((FEAT, COLS), BF16),
                 pltpu.VMEM((3, ROWS, D), F32),
-                pltpu.VMEM((NW, ROWS, COLS), F32),
-                pltpu.VMEM((NW, ROWS, COLS), F32),
-                pltpu.VMEM((2, NW, ROWS, COLS), BF16),
-                pltpu.VMEM((2, NW, ROWS, COLS), BF16),
+                pltpu.VMEM((NW, ROWS + 16, MAIN), BF16),
+                pltpu.VMEM((NW, ROWS + 16, MAIN), BF16),
+                pltpu.VMEM((2, NW, ROWS + 16, MAIN), BF16),
+                pltpu.VMEM((2, NW, ROWS + 16, MAIN), BF16),
                 dma((3,)),
                 dma((NW,)),
                 dma((NW,)),

time: 56.7 us -> 53.6 us (0.945)
  the two profiles are of different devices: /device:TPU:57 before, /device:TPU:1 now
where the time goes in v6:
time: 53.6 us; the launch traced here: 53.4 us
  Pallas kernels  50.8 us (95%)
  between operations  1.93 us (4%)
  local copies, waits for them, and re-layouts  0.73 us (1%)
    pallas_call x1, Pallas kernels, body(): pl.pallas_call(functools.partial(kernel, chips), out_shape=shape, in_spec...  50.8 us

profile of v6, /device:TPU:1, one launch (start us, length us, event | category | flops | bytes accessed | tf_op | source)
XLA Modules:
  0.0 53.4 jit_solution(14097821205717991301)
XLA Ops:
  1.9 50.8 %shard_map.68 = f32[288,256]{1,0:T(8,128)S(1)} custom-call(bf16[144,256]{1,0:T(8,128)(2,1)} %img_hbm.1, bf16[144,256]{1,0:T(8,128)(2,1)} %txt_hbm.1, s32[12]{0:T(128)} %offsets_hbm.1, f32[1]{0:T(128)S(6)} %copy.7.log_scale, f32[1]{0:T(128)S(6)} %copy.8.bias), custom_call_target="tpu_custom_call" | custom-call | tf_op jit(solution)/shard_map/pallas_call | solution.py:502
  52.7 0.7 %fusion = (f32[144,256]{1,0:T(8,128)}, f32[144,256]{1,0:T(8,128)}) fusion(f32[288,256]{1,0:T(8,128)S(1)} %shard_map.68), kind=kLoop, calls=%fused_computation | loop fusion | bytes 589824 | tf_op jit(solution)/shard_map/slice | solution.py:560

commit v7 on v6

--- a/solution.py
+++ b/solution.py
@@ -113,9 +113,19 @@
         )
 
     barrier = pltpu.get_barrier_semaphore()
-    peers = [along(d) for d in (5, -5, 2, -2, 1, -1)] + [across(j) for j in range(1, NW)] + [other]
-    for peer in peers:
+
+    def arrive(peer):
         pl.semaphore_signal(barrier, inc=1, device_id=peer, device_id_type=MESH)
+
+    for d in (-5, -2, -1):
+        arrive(along(d))
+    for j in range(1, NW):
+        arrive(across(j))
+    arrive(other)
+
+    @pl.when(y != NY - 1)
+    def _():
+        arrive(along(1))
 
     get_txt = pltpu.make_async_copy(txt_hbm, txt_in, local_sem.at[0])
     get_img = pltpu.make_async_copy(img_hbm, img_raw.at[w], local_sem.at[1])
@@ -135,7 +145,7 @@
     a_send[...] = txt_wide[...].T.astype(BF16).reshape(NW, ROWS, COLS)
     get_img.wait()
     get_offsets.wait()
-    pl.semaphore_wait(barrier, len(peers))
+    pl.semaphore_wait(barrier, jnp.where(first, NW + 3, NW + 4))
 
     z_copy = remote(img_raw.at[w], img_raw.at[w], b_ss.at[0], b_rs.at[0], partner)
     z_copy.start()
@@ -190,37 +200,41 @@
         copy.start()
         b_copies.append(copy)
 
-    to2.wait_recv()
     to1 = pass_text(2, 1, along(-1))
     to3 = pass_text(2, 3, along(1))
-
-    @pl.when(y != 0)
-    def _():
-        to1.start()
-
-    @pl.when(y != NY - 1)
-    def _():
-        to3.start()
-
-    @pl.when(y == NY - 3)
-    def _():
-        to4_last.start()
-
-    to5.wait_recv()
     to4 = pass_text(5, 4, along(-1))
     to6 = pass_text(5, 6, along(1))
 
-    @pl.when(y != 0)
-    def _():
-        to4.start()
-
-    @pl.when(core == 1)
-    def _():
-        to6.start()
-
-    @pl.when(y == 2)
-    def _():
-        to3_first.start()
+    def forward():
+        to2.wait_recv()
+
+        @pl.when(y != 0)
+        def _():
+            to1.start()
+
+        @pl.when(y != NY - 1)
+        def _():
+            to3.start()
+
+        @pl.when(y == NY - 3)
+        def _():
+            to4_last.start()
+
+        to5.wait_recv()
+
+        @pl.when(y != 0)
+        def _():
+            to4.start()
+
+        @pl.when(core == 1)
+        def _():
+            to6.start()
+
+        @pl.when(y == 2)
+        def _():
+            to3_first.start()
+
+    pl.when(core == 1)(forward)
 
     def squares(v):
         return jnp.sum(jnp.square(img_raw[v].astype(F32)), axis=0, keepdims=True)
@@ -237,6 +251,8 @@
         low[core, NW * MAIN + v * TAIL : NW * MAIN + (v + 1) * TAIL, :] = scaled[MAIN:]
     share = remote(low.at[core], low.at[core], s_ss.at[0], s_rs.at[0], other)
     share.start()
+
+    pl.when(core == 0)(forward)
 
     temper = jnp.exp(jnp.full((1, COLS), log_scale[0], F32))
     shift = bias[0]
@@ -384,10 +400,17 @@
         for n, start in ((NX, base2), (0, base))
         for j in (1, 3, 2)
     ]
-    for copy in e_copies[:3]:
+    for copy in e_copies:
         copy.start()
 
     h_copies = []
+    for t, d in ((0, 5), (1, 2)):
+        owner = lax.rem(chip - d + chips, chips) * 2 + core
+        for j in range(NW):
+            to = lax.rem(w + j, NW)
+            h_copies.append(
+                remote(h_send.at[t, to], h_recv.at[t, w], h_ss.at[t, j], h_rs.at[t, j], (owner, to))
+            )
 
     def send_home(t, d, part):
         text = txt[rows_of(d), :].astype(F32)
@@ -398,55 +421,57 @@
             h_send[t, v, ROWS:, :] = rest
 
         pieces(part, jnp.zeros((8, MAIN), F32), to_home)
-        owner = lax.rem(chip - d + chips, chips) * 2 + core
-        for j in range(NW):
-            to = lax.rem(w + j, NW)
-            copy = remote(h_send.at[t, to], h_recv.at[t, w], h_ss.at[t, j], h_rs.at[t, j], (owner, to))
+        for copy in h_copies[t * NW : (t + 1) * NW]:
             copy.start()
-            h_copies.append(copy)
-
-    @pl.when(y != 0)
-    def _():
-        add_part(PLACE[5], 4)
-
-    @pl.when(core == 1)
-    def _():
-        add_part(PLACE[5], 6)
-
-    @pl.when(y == 2)
-    def _():
-        add_part(PLACE[5], 5)
-
-    send_home(0, 5, keep[PLACE[5]])
-
-    @pl.when(y != 0)
-    def _():
-        add_part(PLACE[2], 1)
-
-    @pl.when(y != NY - 1)
-    def _():
-        add_part(PLACE[2], 3)
-
-    @pl.when(y == NY - 3)
-    def _():
-        add_part(PLACE[2], 2)
-
-    send_home(1, 2, keep[PLACE[2]])
+
+    def text_sums():
+        @pl.when(y != 0)
+        def _():
+            add_part(PLACE[5], 4)
+
+        @pl.when(core == 1)
+        def _():
+            add_part(PLACE[5], 6)
+
+        @pl.when(y == 2)
+        def _():
+            add_part(PLACE[5], 5)
+
+        send_home(0, 5, keep[PLACE[5]])
+
+        @pl.when(y != 0)
+        def _():
+            add_part(PLACE[2], 1)
+
+        @pl.when(y != NY - 1)
+        def _():
+            add_part(PLACE[2], 3)
+
+        @pl.when(y == NY - 3)
+        def _():
+            add_part(PLACE[2], 2)
+
+        send_home(1, 2, keep[PLACE[2]])
+
+    z_back = remote(z_send, z_recv, z_ss.at[0], z_rs.at[0], partner)
+
+    def image_sums():
+        grad = p_own[w2]
+        for j, copy in zip((1, 3, 2), e_copies[:3]):
+            copy.wait_recv()
+            grad = grad + e_recv[NX + j].astype(F32)
+        z_send[...] = grad.astype(BF16)
+        z_back.start()
+
+    pl.when(core == 1)(image_sums)
+    text_sums()
+    pl.when(core == 0)(image_sums)
 
     @pl.when(y == NY - 2)
     def _():
         add_part(PLACE[0], 0)
         send_own()
 
-    grad = p_own[w2]
-    for j, copy in zip((1, 3, 2), e_copies[:3]):
-        copy.wait_recv()
-        grad = grad + e_recv[NX + j].astype(F32)
-    z_send[...] = grad.astype(BF16)
-    z_back = remote(z_send, z_recv, z_ss.at[0], z_rs.at[0], partner)
-    z_back.start()
-    for copy in e_copies[3:]:
-        copy.start()
     grad = p_own[w]
     for j, copy in zip((1, 3, 2), e_copies[3:]):
         copy.wait_recv()

time: 53.6 us -> 53 us (0.989)
  Pallas kernels: 50.8 us -> 50.2 us
    pallas_call x1, Pallas kernels: 50.8 us -> 50.2 us  [body(): pl.pallas_call(functools.partial(kernel, chips), out_shape=shape, in_spec...]
where the time goes in v7:
time: 53 us; the launch traced here: 52.8 us
  Pallas kernels  50.2 us (95%)
  between operations  1.93 us (4%)
  local copies, waits for them, and re-layouts  0.73 us (1%)
    pallas_call x1, Pallas kernels, body(): pl.pallas_call(functools.partial(kernel, chips), out_shape=shape, in_spec...  50.2 us

profile of v7, /device:TPU:1, one launch (start us, length us, event | category | flops | bytes accessed | tf_op | source)
XLA Modules:
  0.0 52.8 jit_solution(10485031972442149415)
XLA Ops:
  1.9 50.2 %shard_map.68 = f32[288,256]{1,0:T(8,128)S(1)} custom-call(bf16[144,256]{1,0:T(8,128)(2,1)} %img_hbm.1, bf16[144,256]{1,0:T(8,128)(2,1)} %txt_hbm.1, s32[12]{0:T(128)} %offsets_hbm.1, f32[1]{0:T(128)S(6)} %copy.7.log_scale, f32[1]{0:T(128)S(6)} %copy.8.bias), custom_call_target="tpu_custom_call" | custom-call | tf_op jit(solution)/shard_map/pallas_call | solution.py:527
  52.1 0.7 %fusion = (f32[144,256]{1,0:T(8,128)}, f32[144,256]{1,0:T(8,128)}) fusion(f32[288,256]{1,0:T(8,128)S(1)} %shard_map.68), kind=kLoop, calls=%fused_computation | loop fusion | bytes 589824 | tf_op jit(solution)/shard_map/slice | solution.py:585

commit v8 on v7

--- a/solution.py
+++ b/solution.py
@@ -187,7 +187,6 @@
     to2.start()
     to1_last = pass_text(0, 1, along(1), 0)
     to4_last = pass_text(2, 4, along(2), 0)
-    to3_first = pass_text(5, 3, along(-2), 0)
 
     @pl.when(y == NY - 2)
     def _():
@@ -212,9 +211,7 @@
         def _():
             to1.start()
 
-        @pl.when(y != NY - 1)
-        def _():
-            to3.start()
+        to3.start()
 
         @pl.when(y == NY - 3)
         def _():
@@ -229,10 +226,6 @@
         @pl.when(core == 1)
         def _():
             to6.start()
-
-        @pl.when(y == 2)
-        def _():
-            to3_first.start()
 
     pl.when(core == 1)(forward)
 
@@ -494,18 +487,16 @@
 
     for copy in a_copies + b_copies + e_copies + g_copies + h_copies:
         copy.wait_send()
-    for copy in (to2, to5, share, pair, z_copy, z_back):
+    for copy in (to2, to3, to5, share, pair, z_copy, z_back):
         copy.wait_send()
     for d in (1, 3, 4):
         back(d).wait_send()
 
     for here, copy in (
         (y != 0, to1),
-        (y != NY - 1, to3),
         (y != 0, to4),
         (y == NY - 2, to1_last),
         (y == NY - 3, to4_last),
-        (y == 2, to3_first),
     ):
         pl.when(here)(copy.wait_send)
 

time: 53 us -> 52.4 us (0.989)
  Pallas kernels: 50.2 us -> 49.6 us
    pallas_call x1, Pallas kernels: 50.2 us -> 49.6 us  [body(): pl.pallas_call(functools.partial(kernel, chips), out_shape=shape, in_spec...]
where the time goes in v8:
time: 52.4 us; the launch traced here: 52.3 us
  Pallas kernels  49.6 us (95%)
  between operations  1.93 us (4%)
  local copies, waits for them, and re-layouts  0.73 us (1%)
    pallas_call x1, Pallas kernels, body(): pl.pallas_call(functools.partial(kernel, chips), out_shape=shape, in_spec...  49.6 us

profile of v8, /device:TPU:1, one launch (start us, length us, event | category | flops | bytes accessed | tf_op | source)
XLA Modules:
  0.0 52.3 jit_solution(17330888619317566134)
XLA Ops:
  1.9 49.6 %shard_map.68 = f32[288,256]{1,0:T(8,128)S(1)} custom-call(bf16[144,256]{1,0:T(8,128)(2,1)} %img_hbm.1, bf16[144,256]{1,0:T(8,128)(2,1)} %txt_hbm.1, s32[12]{0:T(128)} %offsets_hbm.1, f32[1]{0:T(128)S(6)} %copy.7.log_scale, f32[1]{0:T(128)S(6)} %copy.8.bias), custom_call_target="tpu_custom_call" | custom-call | tf_op jit(solution)/shard_map/pallas_call | solution.py:518
  51.5 0.7 %fusion = (f32[144,256]{1,0:T(8,128)}, f32[144,256]{1,0:T(8,128)}) fusion(f32[288,256]{1,0:T(8,128)S(1)} %shard_map.68), kind=kLoop, calls=%fused_computation | loop fusion | bytes 589824 | tf_op jit(solution)/shard_map/slice | solution.py:576

commit v9 on v8

--- a/solution.py
+++ b/solution.py
@@ -112,6 +112,11 @@
             src_ref=src, dst_ref=dst, send_sem=ss, recv_sem=rs, device_id=to, device_id_type=MESH
         )
 
+    get_txt = pltpu.make_async_copy(txt_hbm, txt_in, local_sem.at[0])
+    get_img = pltpu.make_async_copy(img_hbm, img_raw.at[w], local_sem.at[1])
+    get_txt.start()
+    get_img.start()
+
     barrier = pltpu.get_barrier_semaphore()
 
     def arrive(peer):
@@ -127,10 +132,6 @@
     def _():
         arrive(along(1))
 
-    get_txt = pltpu.make_async_copy(txt_hbm, txt_in, local_sem.at[0])
-    get_img = pltpu.make_async_copy(img_hbm, img_raw.at[w], local_sem.at[1])
-    get_txt.start()
-    get_img.start()
     get_offsets = pltpu.make_async_copy(offsets_hbm, offsets, local_sem.at[2])
     get_offsets.start()
 
@@ -388,11 +389,12 @@
     for v in range(NW):
         p_own[v] = p_own[v] + p_recv[v].astype(F32)
         e_send[v] = p_own[v].astype(BF16)
-    e_copies = [
-        remote(e_send.at[start + near(j)], e_recv.at[n + j], e_ss.at[n + j], e_rs.at[n + j], (dp, base + near(j)))
-        for n, start in ((NX, base2), (0, base))
-        for j in (1, 3, 2)
-    ]
+    def along_x(piece, slot, j):
+        return remote(e_send.at[piece], e_recv.at[slot], e_ss.at[slot], e_rs.at[slot], (dp, base + near(j)))
+
+    e_copies = [along_x(base2 + near(j), NX + j, j) for j in (1, 3, 2)]
+    e_copies += [along_x(base + near(1), 1, 1), along_x(base + near(2), 2, 3)]
+    e_last = along_x(base + near(3), 3, 3)
     for copy in e_copies:
         copy.start()
 
@@ -459,6 +461,9 @@
     pl.when(core == 1)(image_sums)
     text_sums()
     pl.when(core == 0)(image_sums)
+    e_copies[4].wait_recv()
+    e_send[base + near(3)] = (p_own[base + near(3)] + e_recv[2].astype(F32)).astype(BF16)
+    e_last.start()
 
     @pl.when(y == NY - 2)
     def _():
@@ -466,7 +471,7 @@
         send_own()
 
     grad = p_own[w]
-    for j, copy in zip((1, 3, 2), e_copies[3:]):
+    for j, copy in ((1, e_copies[3]), (3, e_last)):
         copy.wait_recv()
         grad = grad + e_recv[j].astype(F32)
     z_back.wait_recv()
@@ -487,7 +492,7 @@
 
     for copy in a_copies + b_copies + e_copies + g_copies + h_copies:
         copy.wait_send()
-    for copy in (to2, to3, to5, share, pair, z_copy, z_back):
+    for copy in (to2, to3, to5, share, pair, z_copy, z_back, e_last):
         copy.wait_send()
     for d in (1, 3, 4):
         back(d).wait_send()

time: 52.4 us -> 52.5 us (level)
  no operation moved by 1% of the time
where the time goes in v9:
time: 52.5 us; the launch traced here: 52.3 us
  Pallas kernels  49.6 us (94%)
  between operations  1.93 us (4%)
  local copies, waits for them, and re-layouts  0.73 us (1%)
    pallas_call x1, Pallas kernels, body(): pl.pallas_call(functools.partial(kernel, chips), out_shape=shape, in_spec...  49.6 us

profile of v9, /device:TPU:1, one launch (start us, length us, event | category | flops | bytes accessed | tf_op | source)
XLA Modules:
  0.0 52.3 jit_solution(11809881414301823359)
XLA Ops:
  1.9 49.6 %shard_map.68 = f32[288,256]{1,0:T(8,128)S(1)} custom-call(bf16[144,256]{1,0:T(8,128)(2,1)} %img_hbm.1, bf16[144,256]{1,0:T(8,128)(2,1)} %txt_hbm.1, s32[12]{0:T(128)} %offsets_hbm.1, f32[1]{0:T(128)S(6)} %copy.7.log_scale, f32[1]{0:T(128)S(6)} %copy.8.bias), custom_call_target="tpu_custom_call" | custom-call | tf_op jit(solution)/shard_map/pallas_call | solution.py:523
  51.5 0.7 %fusion = (f32[144,256]{1,0:T(8,128)}, f32[144,256]{1,0:T(8,128)}) fusion(f32[288,256]{1,0:T(8,128)S(1)} %shard_map.68), kind=kLoop, calls=%fused_computation | loop fusion | bytes 589824 | tf_op jit(solution)/shard_map/slice | solution.py:581

commit v10 on v9

--- a/solution.py
+++ b/solution.py
@@ -419,7 +419,7 @@
         for copy in h_copies[t * NW : (t + 1) * NW]:
             copy.start()
 
-    def text_sums():
+    def far_sums():
         @pl.when(y != 0)
         def _():
             add_part(PLACE[5], 4)
@@ -434,6 +434,7 @@
 
         send_home(0, 5, keep[PLACE[5]])
 
+    def near_sums():
         @pl.when(y != 0)
         def _():
             add_part(PLACE[2], 1)
@@ -458,8 +459,9 @@
         z_send[...] = grad.astype(BF16)
         z_back.start()
 
+    far_sums()
     pl.when(core == 1)(image_sums)
-    text_sums()
+    near_sums()
     pl.when(core == 0)(image_sums)
     e_copies[4].wait_recv()
     e_send[base + near(3)] = (p_own[base + near(3)] + e_recv[2].astype(F32)).astype(BF16)

time: 52.5 us -> 52.3 us (level)
  Pallas kernels: 49.6 us -> 49 us
    pallas_call x1, Pallas kernels: 49.6 us -> 49 us  [body(): pl.pallas_call(functools.partial(kernel, chips), out_shape=shape, in_spec...]
where the time goes in v10:
time: 52.3 us; the launch traced here: 51.7 us
  Pallas kernels  49 us (94%)
  between operations  1.93 us (4%)
  local copies, waits for them, and re-layouts  0.73 us (1%)
    pallas_call x1, Pallas kernels, body(): pl.pallas_call(functools.partial(kernel, chips), out_shape=shape, in_spec...  49 us

profile of v10, /device:TPU:1, one launch (start us, length us, event | category | flops | bytes accessed | tf_op | source)
XLA Modules:
  0.0 51.7 jit_solution(4447230478520412324)
XLA Ops:
  1.9 49.0 %shard_map.68 = f32[288,256]{1,0:T(8,128)S(1)} custom-call(bf16[144,256]{1,0:T(8,128)(2,1)} %img_hbm.1, bf16[144,256]{1,0:T(8,128)(2,1)} %txt_hbm.1, s32[12]{0:T(128)} %offsets_hbm.1, f32[1]{0:T(128)S(6)} %copy.7.log_scale, f32[1]{0:T(128)S(6)} %copy.8.bias), custom_call_target="tpu_custom_call" | custom-call | tf_op jit(solution)/shard_map/pallas_call | solution.py:525
  50.9 0.7 %fusion = (f32[144,256]{1,0:T(8,128)}, f32[144,256]{1,0:T(8,128)}) fusion(f32[288,256]{1,0:T(8,128)S(1)} %shard_map.68), kind=kLoop, calls=%fused_computation | loop fusion | bytes 589824 | tf_op jit(solution)/shard_map/slice | solution.py:583

commit v11 on v10

--- a/solution.py
+++ b/solution.py
@@ -256,7 +256,7 @@
 
     home = {
         1: (jnp.where(last, -1, 1), jnp.where(last, 0, 1)),
-        3: (jnp.where(first, 2, -1), jnp.where(first, 5, 3)),
+        3: (-1, 3),
         4: (jnp.where(last, -2, 1), jnp.where(last, 2, 4)),
         6: (-1, 6),
     }
@@ -428,10 +428,6 @@
         def _():
             add_part(PLACE[5], 6)
 
-        @pl.when(y == 2)
-        def _():
-            add_part(PLACE[5], 5)
-
         send_home(0, 5, keep[PLACE[5]])
 
     def near_sums():
@@ -439,9 +435,7 @@
         def _():
             add_part(PLACE[2], 1)
 
-        @pl.when(y != NY - 1)
-        def _():
-            add_part(PLACE[2], 3)
+        add_part(PLACE[2], 3)
 
         @pl.when(y == NY - 3)
         def _():

time: 52.3 us -> 52.3 us (level)
  no operation moved by 1% of the time
where the time goes in v11:
time: 52.3 us; the launch traced here: 52.1 us
  Pallas kernels  49.5 us (95%)
  between operations  1.93 us (4%)
  local copies, waits for them, and re-layouts  0.73 us (1%)
    pallas_call x1, Pallas kernels, body(): pl.pallas_call(functools.partial(kernel, chips), out_shape=shape, in_spec...  49.5 us

profile of v11, /device:TPU:1, one launch (start us, length us, event | category | flops | bytes accessed | tf_op | source)
XLA Modules:
  0.0 52.1 jit_solution(7617499353821953353)
XLA Ops:
  1.9 49.5 %shard_map.68 = f32[288,256]{1,0:T(8,128)S(1)} custom-call(bf16[144,256]{1,0:T(8,128)(2,1)} %img_hbm.1, bf16[144,256]{1,0:T(8,128)(2,1)} %txt_hbm.1, s32[12]{0:T(128)} %offsets_hbm.1, f32[1]{0:T(128)S(6)} %copy.7.log_scale, f32[1]{0:T(128)S(6)} %copy.8.bias), custom_call_target="tpu_custom_call" | custom-call | tf_op jit(solution)/shard_map/pallas_call | solution.py:519
  51.4 0.7 %fusion = (f32[144,256]{1,0:T(8,128)}, f32[144,256]{1,0:T(8,128)}) fusion(f32[288,256]{1,0:T(8,128)S(1)} %shard_map.68), kind=kLoop, calls=%fused_computation | loop fusion | bytes 589824 | tf_op jit(solution)/shard_map/slice | solution.py:577
